TPU v7x, 128 devices: a whole 4x4x4 slice. The times are simulated.
128 devices in a mesh: lon: 16 (over z, x_hi, core), lat: 8 (over y, x_lo).
Axes of the slice: x: 4 (x_hi: 2, x_lo: 2; x = x_hi * 2 + x_lo), y: 4, z: 4, core: 2. Of those that a mesh axis runs over, the one named last changes fastest.
Arguments:
- stream: bfloat16 [192, 144, 4, 512], P('lon', 'lat'), may hold values from -6 to 6
- w_qkv: bfloat16 [2, 512, 1536], replicated, may hold values from -8 to 8
- w_out: bfloat16 [2, 512, 512], replicated, may hold values from -0.25 to 0.25
- w_up: bfloat16 [2, 512, 2048], replicated, may hold values from -0.25 to 0.25
- w_down: bfloat16 [2, 2048, 512], replicated, may hold values from -0.125 to 0.125
- block_gains: float32 [2, 2, 512], replicated, may hold values from 0.1 to 1.9
- merge_gain: float32 [2048], replicated, may hold values from 0.1 to 1.9
- w_merge: bfloat16 [2048, 1024], replicated, may hold values from -0.125 to 0.125
Outputs:
- merged: bfloat16 [96, 72, 4, 1024], P('lon', 'lat')
All inputs are finite; a program needn't handle non-finite values.
Results may differ from a plain program's by a relative error of at most 0.022.
Values may be sent and summed in bfloat16 or wider, within the bound.
No kernel may reach another device: no remote copies, remote signals or barrier semaphores. Data moves between devices by JAX's collectives and lax.ppermute only.
A program may use at most 256 MiB of HBM per device.

v0:
```python
import functools

import jax
import jax.numpy as jnp
from jax import lax
from jax.experimental import pallas as pl
from jax.experimental.pallas import tpu as pltpu
from jax.sharding import PartitionSpec as P

EPSILON = 1e-05
D = 512
FF = 2048
COLS, ROWS, LEV = 12, 18, 4
HALF = 432
ALL = 864
WIN = 144
F32 = jnp.float32
BF16 = jnp.bfloat16
VMEM_LIMIT = 44 * 1024 * 1024


def norm_rows(values, gain):
    center = jnp.mean(values, axis=-1, keepdims=True)
    off = values - center
    spread = jnp.mean(off * off, axis=-1, keepdims=True)
    return off * lax.rsqrt(spread + EPSILON) * gain


def round_bf16(values):
    return values.astype(BF16).astype(F32)


def mm(a, b):
    return jnp.dot(a, b, preferred_element_type=F32)


def gelu(x):
    inner = 0.7978845608028654 * (x + 0.044715 * (x * x * x))
    return 0.5 * x * (1.0 + jnp.tanh(inner))


def attend_unit(packed_ref, row0, group, mask):
    span = pl.ds(row0, WIN)
    lo = group * 256
    q = packed_ref[span, lo : lo + 256] * jnp.asarray(0.125, BF16)
    k = packed_ref[span, D + lo : D + lo + 256]
    v = packed_ref[span, 2 * D + lo : 2 * D + lo + 256]
    lane = lax.broadcasted_iota(jnp.int32, (WIN, 256), 1) // 64
    zero = jnp.zeros_like(q)
    stacked = jnp.concatenate([jnp.where(lane == h, q, zero) for h in range(4)], axis=0)
    scores = lax.dot_general(k, stacked, (((1,), (1,)), ((), ())), preferred_element_type=F32)
    if mask is not None:
        scores = jnp.where(mask, scores, -1e30)
    peak = jnp.max(scores, axis=0, keepdims=True)
    e = jnp.exp(scores - peak)
    weights = (e * (1.0 / jnp.sum(e, axis=0, keepdims=True))).astype(BF16)
    mixed = lax.dot_general(weights, v, (((0,), (0,)), ((), ())), preferred_element_type=F32)
    out = mixed[0:WIN]
    for h in range(1, 4):
        out = jnp.where(lane == h, mixed[h * WIN : (h + 1) * WIN], out)
    return out


def finish_rows(stream, attended, wo, wu, wd, gain):
    middle = round_bf16(stream + mm(attended, wo[...]))
    hidden_in = norm_rows(middle, gain).astype(BF16)
    total = middle
    for c in range(4):
        raised = mm(hidden_in, wu[:, c * 512 : (c + 1) * 512])
        total = total + mm(gelu(raised).astype(BF16), wd[c * 512 : (c + 1) * 512, :])
    return round_bf16(total)


def put_rows(ref, start, values):
    for j in range(4):
        ref[j, start : start + values.shape[0], :] = values[:, j * 128 : (j + 1) * 128]


def gather_windows(src, dst, levels):
    for w in range(6):
        for j in range(4):
            pieces = [src[j, pl.ds((w % 3) * 288 + level, 72, stride=4), :] for level in levels[w // 3]]
            dst[w * WIN : (w + 1) * WIN, j * 128 : (j + 1) * 128] = jnp.concatenate(pieces, axis=0).astype(BF16)


def windows_attention(packed, att, levels, masks):
    for w in range(6):
        for group in range(2):
            out = attend_unit(packed, w * WIN, group, masks[w])
            for part, level in enumerate(levels[w // 3]):
                for j in range(2):
                    att[group * 2 + j, pl.ds((w % 3) * 288 + level, 72, stride=4), :] = out[
                        part * 72 : (part + 1) * 72, j * 128 : (j + 1) * 128
                    ]


def half_of(ref, which):
    pieces = [ref[j].reshape(ROWS, 48, 128)[:, which * 24 : which * 24 + 24].reshape(HALF, 128) for j in range(4)]
    return jnp.concatenate(pieces, axis=1)


def load(hbm, vmem, sem):
    copy = pltpu.make_async_copy(hbm, vmem, sem)
    copy.start()
    return copy


def first_kernel(x, wqkv_h, wo_h, wu_h, wd_h, gains, first_a, normed_a, x_b, att_b,
                 xs, ns, nw, packed, wqkv, wo, wu, wd, sems):
    copies = [load(h.at[0], v, sems.at[i])
              for i, (h, v) in enumerate(((wqkv_h, wqkv), (wo_h, wo), (wu_h, wu), (wd_h, wd)))]
    for r in range(ROWS):
        for p in range(6):
            pair = jnp.concatenate([x[2 * p, r].astype(F32), x[2 * p + 1, r].astype(F32)], axis=0)
            put_rows(xs, r * 48 + p * 8, pair)
    put_rows(ns, 0, norm_rows(jnp.concatenate([xs[j] for j in range(4)], axis=1), gains[0, 0:1]))
    gather_windows(ns, nw, ((0, 1), (2, 3)))
    copies[0].wait()
    for c in range(3):
        packed[:, c * 512 : (c + 1) * 512] = mm(nw[...], wqkv[:, c * 512 : (c + 1) * 512]).astype(BF16)
    windows_attention(packed, ns, ((0, 1), (2, 3)), [None] * 6)
    x_b[...] = half_of(xs, 1).astype(BF16)
    att_b[...] = half_of(ns, 1).astype(BF16)
    for copy in copies[1:]:
        copy.wait()
    result = finish_rows(half_of(xs, 0), half_of(ns, 0).astype(BF16), wo, wu, wd, gains[0, 1:2])
    first_a[...] = result.astype(BF16)
    normed_a[...] = norm_rows(result, gains[1, 0:1]).astype(BF16)


def second_kernel(x_b, att_b, wo_h, wu_h, wd_h, gains, first_b, normed_b, wo, wu, wd, sems):
    copies = [load(h.at[0], v, sems.at[i]) for i, (h, v) in enumerate(((wo_h, wo), (wu_h, wu), (wd_h, wd)))]
    for copy in copies:
        copy.wait()
    result = finish_rows(x_b[...].astype(F32), att_b[...], wo, wu, wd, gains[0, 1:2])
    first_b[...] = result.astype(BF16)
    normed_b[...] = norm_rows(result, gains[1, 0:1]).astype(BF16)


def third_kernel(bottom, n_b, n_ra, halo, wqkv_h, z_b, z_ra, ns, nw, packed, wqkv, sems):
    copy = load(wqkv_h.at[1], wqkv, sems.at[0])
    for which, ref in enumerate((n_b, n_ra)):
        rows = ref[...].astype(F32).reshape(ROWS, 24, D)
        extra = halo[...].astype(F32)[which * 72 : (which + 1) * 72].reshape(3, 24, D)
        for r in range(ROWS):
            at = r * 48 + which * 24
            put_rows(ns, at, rows[r + 3] if r < 15 else extra[r - 15])
    levels = ((1, 2), (3, 0))
    gather_windows(ns, nw, levels)
    copy.wait()
    for c in range(3):
        packed[:, c * 512 : (c + 1) * 512] = mm(nw[...], wqkv[:, c * 512 : (c + 1) * 512]).astype(BF16)
    key = lax.broadcasted_iota(jnp.int32, (WIN, 4 * WIN), 0)
    query = lax.rem(lax.broadcasted_iota(jnp.int32, (WIN, 4 * WIN), 1), WIN)
    same_level = (key < 72) == (query < 72)
    same_side = ((lax.rem(key, 72) < 36) == (lax.rem(query, 72) < 36)) | (bottom[0] == 0)
    masks = [None, None, same_side, same_level, same_level, same_level & same_side]
    windows_attention(packed, ns, levels, masks)
    z_b[...] = half_of(ns, 0).astype(BF16)
    z_ra[...] = half_of(ns, 1).astype(BF16)


def fourth_kernel(f_a, f_b, att_a, att_b, wo_h, wu_h, wd_h, gains, merge_gain, wm_h, out,
                  wo, wu, wd, wm, sems):
    copies = [load(h, v, sems.at[i]) for i, (h, v) in enumerate(
        ((wo_h.at[1], wo), (wu_h.at[1], wu), (wd_h.at[1], wd), (wm_h, wm)))]
    for copy in copies[:3]:
        copy.wait()
    s_b = finish_rows(f_b[...].astype(F32), att_b[...], wo, wu, wd, gains[1, 1:2]).reshape(9, 2, 3, 8, D)
    s_a = finish_rows(f_a[...].astype(F32), att_a[...], wo, wu, wd, gains[1, 1:2]).reshape(9, 2, 3, 8, D)
    top = lax.broadcasted_iota(jnp.int32, (216, D), 0) % 8 < 4
    parts = []
    for rp in range(2):
        a = s_a[:, rp].reshape(216, D)
        b = s_b[:, rp].reshape(216, D)
        a_turned = pltpu.roll(a.reshape(27, 8, D), 4, 1).reshape(216, D)
        b_turned = pltpu.roll(b.reshape(27, 8, D), 4, 1).reshape(216, D)
        parts.append(jnp.where(top, a, b_turned))
        parts.append(jnp.where(top, a_turned, b))
    center = sum(jnp.sum(p, axis=-1, keepdims=True) for p in parts) * (1.0 / 2048)
    parts = [p - center for p in parts]
    spread = sum(jnp.sum(p * p, axis=-1, keepdims=True) for p in parts) * (1.0 / 2048)
    scale = lax.rsqrt(spread + EPSILON)
    copies[3].wait()
    total = None
    for i, p in enumerate(parts):
        normed = (p * scale * merge_gain[0:1, i * 512 : (i + 1) * 512]).astype(BF16)
        term = mm(normed, wm[i * 512 : (i + 1) * 512, :])
        total = term if total is None else total + term
    out[...] = total.astype(BF16)


ANY = pl.BlockSpec(memory_space=pl.ANY)
VM = pl.BlockSpec(memory_space=pltpu.VMEM)
SM = pl.BlockSpec(memory_space=pltpu.SMEM)
PARAMS = pltpu.CompilerParams(vmem_limit_bytes=VMEM_LIMIT)


def half_shape():
    return jax.ShapeDtypeStruct((HALF, D), BF16)


FINISH_WEIGHTS = [pltpu.VMEM((D, D), BF16), pltpu.VMEM((D, FF), BF16), pltpu.VMEM((FF, D), BF16)]
ATTENTION_SCRATCH = [pltpu.VMEM((4, ALL, 128), F32), pltpu.VMEM((ALL, D), BF16), pltpu.VMEM((ALL, 3 * D), BF16),
                     pltpu.VMEM((D, 3 * D), BF16)]


def call_first(x, w_qkv, w_out, w_up, w_down, gains):
    return pl.pallas_call(
        first_kernel,
        out_shape=[half_shape()] * 4,
        in_specs=[VM, ANY, ANY, ANY, ANY, VM],
        out_specs=[VM] * 4,
        scratch_shapes=[pltpu.VMEM((4, ALL, 128), F32)] + ATTENTION_SCRATCH + FINISH_WEIGHTS
        + [pltpu.SemaphoreType.DMA((4,))],
        compiler_params=PARAMS,
        name="block_one",
    )(x, w_qkv, w_out, w_up, w_down, gains)


def call_second(x_b, att_b, w_out, w_up, w_down, gains):
    return pl.pallas_call(
        second_kernel,
        out_shape=[half_shape()] * 2,
        in_specs=[VM, VM, ANY, ANY, ANY, VM],
        out_specs=[VM] * 2,
        scratch_shapes=FINISH_WEIGHTS + [pltpu.SemaphoreType.DMA((3,))],
        compiler_params=PARAMS,
        cost_estimate=pl.CostEstimate(flops=4_000_000_000, bytes_accessed=6_000_000, transcendentals=900_000),
        name="block_one_rest",
    )(x_b, att_b, w_out, w_up, w_down, gains)


def call_third(bottom, n_b, n_ra, halo, w_qkv):
    return pl.pallas_call(
        third_kernel,
        out_shape=[half_shape()] * 2,
        in_specs=[SM, VM, VM, VM, ANY],
        out_specs=[VM] * 2,
        scratch_shapes=ATTENTION_SCRATCH + [pltpu.SemaphoreType.DMA((1,))],
        compiler_params=PARAMS,
        name="shifted_attention",
    )(bottom, n_b, n_ra, halo, w_qkv)


def call_fourth(f_a, f_b, att_a, att_b, w_out, w_up, w_down, gains, merge_gain, w_merge):
    return pl.pallas_call(
        fourth_kernel,
        out_shape=jax.ShapeDtypeStruct((216, 1024), BF16),
        in_specs=[VM, VM, VM, VM, ANY, ANY, ANY, VM, VM, ANY],
        out_specs=VM,
        scratch_shapes=FINISH_WEIGHTS + [pltpu.VMEM((4 * D, 1024), BF16), pltpu.SemaphoreType.DMA((4,))],
        compiler_params=PARAMS,
        name="block_two_rest",
    )(f_a, f_b, att_a, att_b, w_out, w_up, w_down, gains, merge_gain, w_merge)


def ring(value, axis, by):
    length = lax.axis_size(axis)
    return lax.ppermute(value, axis, [(i, (i + by) % length) for i in range(length)])


def body(stream, w_qkv, w_out, w_up, w_down, block_gains, merge_gain, w_merge):
    bottom = (lax.axis_index("lat") == lax.axis_size("lat") - 1).astype(jnp.int32).reshape(1)
    first_a, normed_a, x_b, att_b = call_first(stream, w_qkv, w_out, w_up, w_down, block_gains)
    normed_ra = ring(normed_a, "lon", -1)
    first_b, normed_b = call_second(x_b, att_b, w_out, w_up, w_down, block_gains)
    halo = ring(jnp.concatenate([normed_b[:72], normed_ra[:72]], axis=0), "lat", -1)
    z_b, z_ra = call_third(bottom, normed_b, normed_ra, halo, w_qkv)
    back = ring(jnp.concatenate([z_b[360:], z_ra[360:]], axis=0), "lat", 1)
    att_b = jnp.concatenate([back[:72], z_b[:360]], axis=0)
    att_a = ring(jnp.concatenate([back[72:], z_ra[:360]], axis=0), "lon", 1)
    out = call_fourth(first_a, first_b, att_a, att_b, w_out, w_up, w_down, block_gains,
                      merge_gain.reshape(1, -1), w_merge)
    out = out.reshape(9, 3, 2, LEV, 1024).transpose(2, 1, 0, 3, 4)
    return out.reshape(6, 9, LEV, 1024)


def solution(mesh):
    return jax.shard_map(
        body,
        mesh=mesh,
        in_specs=(P("lon", "lat", None, None), P(), P(), P(), P(), P(), P(), P()),
        out_specs=P("lon", "lat", None, None),
        check_vma=False,
    )
```

profile of v0, /device:TPU:0, one launch (start us, length us, event | category | flops | bytes accessed | tf_op | source)
XLA Modules:
  0.0 73.7 jit_solution(9343963345733088205)
XLA Ops:
  0.0 0.0 copy-start
  0.0 0.0 copy-start.2
  0.0 2.0 %copy-done.2 = bf16[2,512,1536]{2,1,0:T(8,128)(2,1)S(1)} copy-done((bf16[2,512,1536]{2,1,0:T(8,128)(2,1)S(1)}, bf16[2,512,1536]{2,1,0:T(8,128)(2,1)}, u32[]{:S(2)}) %copy-start.2) | copy-done | bytes 3145752
  2.0 0.0 copy-start.4
  2.0 1.4 %copy-done.4 = bf16[2,512,512]{2,1,0:T(8,128)(2,1)S(1)} copy-done((bf16[2,512,512]{2,1,0:T(8,128)(2,1)S(1)}, bf16[2,512,512]{2,1,0:T(8,128)(2,1)}, u32[]{:S(2)}) %copy-start.4) | copy-done | bytes 1048600
  3.4 0.0 copy-start.6
  3.4 1.2 %copy-done.6 = bf16[12,18,4,512]{3,2,1,0:T(4,128)(2,1)S(1)} copy-done((bf16[12,18,4,512]{3,2,1,0:T(4,128)(2,1)S(1)}, bf16[12,18,4,512]{3,2,1,0:T(4,128)(2,1)}, u32[]{:S(2)}) %copy-start.6) | copy-done | bytes 884760
  4.6 0.0 copy-start.15
  4.6 0.7 copy-done.15
  5.3 9.8 %block_one.1 = (bf16[432,512]{1,0:T(8,128)(2,1)S(1)}, bf16[432,512]{1,0:T(8,128)(2,1)S(1)}, bf16[432,512]{1,0:T(8,128)(2,1)S(1)}, bf16[432,512]{1,0:T(8,128)(2,1)S(1)}) custom-call(bf16[12,18,4,512]{3,2,1,0:T(4,128)(2,1)S(1)} %copy-done.6, bf16[2,512,1536]{2,1,0:T(8,128)(2,1)S(1)} %copy-done.2, bf16[2,512,512]{2,1,0:T(8,128)(2,1)S(1)} %copy-done.4, ...), custom_call_target="tpu_custom_call" | custom-call | tf_op jit(solution)/shard_map/block_one/pallas_call | solution.py:209
  15.2 0.0 copy-start.11
  15.2 0.8 %copy-done.11 = bf16[432,512]{1,0:T(8,128)(2,1)} copy-done((bf16[432,512]{1,0:T(8,128)(2,1)}, bf16[432,512]{1,0:T(8,128)(2,1)S(1)}, u32[]{:S(2)}) %copy-start.11) | copy-done | bytes 442392
  15.9 6.0 %collective-permute-start = (bf16[432,512]{1,0:T(8,128)(2,1)S(1)}, bf16[432,512]{1,0:T(8,128)(2,1)S(1)}, u32[]{:S(2)}, u32[]{:S(2)}) collective-permute-start(bf16[432,512]{1,0:T(8,128)(2,1)S(1)} %get-tuple-element.18), channel_id=1, source_target_pairs={{0,120},{8,0},{16,8},{24,16},{32,24},{40,32},{48,40},{56,48},{64,5... | collective-permute-start | bytes 1327112 | tf_op jit(solution)/shard_map/ppermute | solution.py:260
  21.9 0.0 copy-done
  21.9 0.0 copy-start.3
  21.9 5.3 %block_one_rest.1 = (bf16[432,512]{1,0:T(8,128)(2,1)S(1)}, bf16[432,512]{1,0:T(8,128)(2,1)S(1)}) custom-call(bf16[432,512]{1,0:T(8,128)(2,1)S(1)} %get-tuple-element.14.x_b, bf16[432,512]{1,0:T(8,128)(2,1)S(1)} %get-tuple-element.15.att_b, bf16[2,512,512]{2,1,0:T(8,128)(2,1)S(1)} %copy-done.4, bf16[2,512,2048]{2,1,0:T(8,128)(2,1)S(1)} %copy-done, ...), custom_call_target="tpu_custom_call" | custom-call | flops 4000000000 | bytes 6000000 | tf_op jit(solution)/shard_map/block_one_rest/pallas_call | solution.py:222
  27.2 0.0 copy-start.13
  27.2 0.8 %copy-done.13 = bf16[432,512]{1,0:T(8,128)(2,1)} copy-done((bf16[432,512]{1,0:T(8,128)(2,1)}, bf16[432,512]{1,0:T(8,128)(2,1)S(1)}, u32[]{:S(2)}) %copy-start.13) | copy-done | bytes 442392
  28.0 0.8 %copy-done.9 = bf16[432,512]{1,0:T(8,128)(2,1)} copy-done((bf16[432,512]{1,0:T(8,128)(2,1)}, bf16[432,512]{1,0:T(8,128)(2,1)S(1)}, u32[]{:S(2)}) %copy-start.9) | copy-done | bytes 442392
  28.8 0.0 collective-permute-done.n_ra
  28.8 0.0 copy-start.7
  28.8 0.8 %copy-done.7 = bf16[432,512]{1,0:T(8,128)(2,1)} copy-done((bf16[432,512]{1,0:T(8,128)(2,1)}, bf16[432,512]{1,0:T(8,128)(2,1)S(1)}, u32[]{:S(2)}) %copy-start.7) | copy-done | bytes 442392
  29.6 0.0 copy-start.17
  29.6 0.0 copy-start.16
  29.6 3.3 %collective-permute-start.1 = (bf16[144,512]{1,0:T(8,128)(2,1)S(1)}, bf16[144,512]{1,0:T(8,128)(2,1)S(1)}, u32[]{:S(2)}, u32[]{:S(2)}) collective-permute-start(bf16[144,512]{1,0:T(8,128)(2,1)S(1)} %pad_maximum_fusion.2), channel_id=1, source_target_pairs={{0,7},{1,0},{2,1},{3,2},{4,3},{5,4},{6,5},{7,6},{8,15},{9,8},{10,9... | collective-permute-start | bytes 442376 | tf_op jit(solution)/shard_map/ppermute | solution.py:260
  32.9 0.0 copy-start.1
  32.9 0.0 copy-start.5
  32.9 2.7 %collective-permute-done.1.halo = bf16[144,512]{1,0:T(8,128)(2,1)S(1)} collective-permute-done((bf16[144,512]{1,0:T(8,128)(2,1)S(1)}, bf16[144,512]{1,0:T(8,128)(2,1)S(1)}, u32[]{:S(2)}, u32[]{:S(2)}) %collective-permute-start.1) | collective-permute-done | bytes 147488 | tf_op jit(solution)/shard_map/ppermute | solution.py:260
  35.6 0.0 copy-done.3
  35.6 0.0 copy-start.8
  35.6 1.0 %copy-done.8 = bf16[432,512]{1,0:T(8,128)(2,1)S(1)} copy-done((bf16[432,512]{1,0:T(8,128)(2,1)S(1)}, bf16[432,512]{1,0:T(8,128)(2,1)}, u32[]{:S(2)}) %copy-start.8) | copy-done | bytes 442392
  36.6 0.0 copy-start.10
  36.6 1.0 %copy-done.10 = bf16[432,512]{1,0:T(8,128)(2,1)S(1)} copy-done((bf16[432,512]{1,0:T(8,128)(2,1)S(1)}, bf16[432,512]{1,0:T(8,128)(2,1)}, u32[]{:S(2)}) %copy-start.10) | copy-done | bytes 442392
  37.6 0.0 copy-start.12
  37.6 6.0 %shifted_attention.1 = (bf16[432,512]{1,0:T(8,128)(2,1)S(1)}, bf16[432,512]{1,0:T(8,128)(2,1)S(1)}) custom-call(s32[1]{0:T(128)} %bitcast.bottom, bf16[432,512]{1,0:T(8,128)(2,1)S(1)} %copy-done.10, bf16[432,512]{1,0:T(8,128)(2,1)S(1)} %copy-done.8, bf16[144,512]{1,0:T(8,128)(2,1)S(1)} %collective-permute-done.1.halo, bf16[2,512,1536]{2,1,0:T(8,128)(2,1)S(1)} %copy-done.3), custom_call_target="tpu_custom_call" | custom-call | tf_op jit(solution)/shard_map/shifted_attention/pallas_call | solution.py:235
  43.7 1.0 %collective-permute-start.2 = (bf16[144,512]{1,0:T(8,128)(2,1)S(1)}, bf16[144,512]{1,0:T(8,128)(2,1)S(1)}, u32[]{:S(2)}, u32[]{:S(2)}) collective-permute-start(bf16[144,512]{1,0:T(8,128)(2,1)S(1)} %pad_maximum_fusion.3), channel_id=1, source_target_pairs={{0,1},{1,2},{2,3},{3,4},{4,5},{5,6},{6,7},{7,0},{8,9},{9,10},{10,1... | collective-permute-start | bytes 442376 | tf_op jit(solution)/shard_map/ppermute | solution.py:260
  44.7 6.8 %collective-permute-done.2 = bf16[144,512]{1,0:T(8,128)(2,1)S(1)} collective-permute-done((bf16[144,512]{1,0:T(8,128)(2,1)S(1)}, bf16[144,512]{1,0:T(8,128)(2,1)S(1)}, u32[]{:S(2)}, u32[]{:S(2)}) %collective-permute-start.2) | collective-permute-done | bytes 147488 | tf_op jit(solution)/shard_map/ppermute | solution.py:260
  51.5 0.3 collective-permute-start.3
  51.9 11.3 %collective-permute-done.3.att_a = bf16[432,512]{1,0:T(8,128)(2,1)S(1)} collective-permute-done((bf16[432,512]{1,0:T(8,128)(2,1)S(1)}, bf16[432,512]{1,0:T(8,128)(2,1)S(1)}, u32[]{:S(2)}, u32[]{:S(2)}) %collective-permute-start.3) | collective-permute-done | bytes 442400 | tf_op jit(solution)/shard_map/ppermute | solution.py:260
  63.1 0.0 copy-done.17
  63.1 0.0 copy-done.16
  63.1 0.0 copy-done.1
  63.1 0.0 copy-done.5
  63.1 0.0 copy-done.12
  63.1 0.0 copy-done.14
  63.2 9.5 %block_two_rest.1 = bf16[216,1024]{1,0:T(8,128)(2,1)S(1)} custom-call(bf16[432,512]{1,0:T(8,128)(2,1)S(1)} %copy-done.12, bf16[432,512]{1,0:T(8,128)(2,1)S(1)} %copy-done.14, bf16[432,512]{1,0:T(8,128)(2,1)S(1)} %collective-permute-done.3.att_a, bf16[432,512]{1,0:T(8,128)(2,1)S(1)} %pad_maximum_fusion.1.att_b, bf16[2,512,512]{2,1,0:T(8,128)(2,1)S(1)} %copy-done.5, ...), custom_call_target="tpu_custom_call" | custom-call | tf_op jit(solution)/shard_map/block_two_rest/pallas_call | solution.py:247
  72.6 0.2 reshape.17
  72.8 0.9 %copy.9 = bf16[2,3,9,4,1024]{4,3,2,1,0:T(4,128)(2,1)} copy(bf16[2,3,9,4,1024]{4,3,0,1,2:T(4,128)(2,1)S(1)} %bitcast.5) | data formatting | bytes 884736 | tf_op jit(solution)/shard_map/transpose | solution.py:275
  (13 shorter events, 0.2 us)
Async XLA Ops:
  0.0 21.9 %copy-start = (bf16[2,512,2048]{2,1,0:T(8,128)(2,1)S(1)}, bf16[2,512,2048]{2,1,0:T(8,128)(2,1)}, u32[]{:S(2)}) copy-start(bf16[2,512,2048]{2,1,0:T(8,128)(2,1)} %wu_h.5) | copy-start | bytes 12582916
  0.0 2.0 %copy-start.2 = (bf16[2,512,1536]{2,1,0:T(8,128)(2,1)S(1)}, bf16[2,512,1536]{2,1,0:T(8,128)(2,1)}, u32[]{:S(2)}) copy-start(bf16[2,512,1536]{2,1,0:T(8,128)(2,1)} %wqkv_h.3) | copy-start | bytes 9437188
  2.0 1.4 %copy-start.4 = (bf16[2,512,512]{2,1,0:T(8,128)(2,1)S(1)}, bf16[2,512,512]{2,1,0:T(8,128)(2,1)}, u32[]{:S(2)}) copy-start(bf16[2,512,512]{2,1,0:T(8,128)(2,1)} %wo_h.5) | copy-start | bytes 3145732
  3.4 1.2 %copy-start.6 = (bf16[12,18,4,512]{3,2,1,0:T(4,128)(2,1)S(1)}, bf16[12,18,4,512]{3,2,1,0:T(4,128)(2,1)}, u32[]{:S(2)}) copy-start(bf16[12,18,4,512]{3,2,1,0:T(4,128)(2,1)} %x.1) | copy-start | bytes 2654212
  4.6 0.7 copy-start.15
  15.2 0.8 %copy-start.11 = (bf16[432,512]{1,0:T(8,128)(2,1)}, bf16[432,512]{1,0:T(8,128)(2,1)S(1)}, u32[]{:S(2)}) copy-start(bf16[432,512]{1,0:T(8,128)(2,1)S(1)} %get-tuple-element.13.f_a) | copy-start | bytes 1327108
  15.9 12.9 %collective-permute-start = (bf16[432,512]{1,0:T(8,128)(2,1)S(1)}, bf16[432,512]{1,0:T(8,128)(2,1)S(1)}, u32[]{:S(2)}, u32[]{:S(2)}) collective-permute-start(bf16[432,512]{1,0:T(8,128)(2,1)S(1)} %get-tuple-element.18), channel_id=1, source_target_pairs={{0,120},{8,0},{16,8},{24,16},{32,24},{40,32},{48,40},{56,48},{64,5... | collective-permute-start | bytes 1327112 | tf_op jit(solution)/shard_map/ppermute | solution.py:260
  21.9 13.7 %copy-start.3 = (bf16[2,512,1536]{2,1,0:T(8,128)(2,1)S(1)}, bf16[2,512,1536]{2,1,0:T(8,128)(2,1)}, u32[]{:S(2)}) copy-start(bf16[2,512,1536]{2,1,0:T(8,128)(2,1)} %wqkv_h.3) | copy-start | bytes 9437188
  27.2 0.8 %copy-start.13 = (bf16[432,512]{1,0:T(8,128)(2,1)}, bf16[432,512]{1,0:T(8,128)(2,1)S(1)}, u32[]{:S(2)}) copy-start(bf16[432,512]{1,0:T(8,128)(2,1)S(1)} %get-tuple-element.16.f_b) | copy-start | bytes 1327108
  28.0 0.8 %copy-start.9 = (bf16[432,512]{1,0:T(8,128)(2,1)}, bf16[432,512]{1,0:T(8,128)(2,1)S(1)}, u32[]{:S(2)}) copy-start(bf16[432,512]{1,0:T(8,128)(2,1)S(1)} %get-tuple-element.17.n_b) | copy-start | bytes 1327108
  28.8 0.8 %copy-start.7 = (bf16[432,512]{1,0:T(8,128)(2,1)}, bf16[432,512]{1,0:T(8,128)(2,1)S(1)}, u32[]{:S(2)}) copy-start(bf16[432,512]{1,0:T(8,128)(2,1)S(1)} %collective-permute-done.n_ra) | copy-start | bytes 1327108
  29.6 33.5 %copy-start.17 = (f32[2048]{0:T(1024)S(1)}, f32[2048]{0:T(1024)}, u32[]{:S(2)}) copy-start(f32[2048]{0:T(1024)} %param.14) | copy-start | bytes 24580
  29.6 33.5 %copy-start.16 = (f32[2,2,512]{2,1,0:T(2,128)S(1)}, f32[2,2,512]{2,1,0:T(2,128)}, u32[]{:S(2)}) copy-start(f32[2,2,512]{2,1,0:T(2,128)} %gains.5) | copy-start | bytes 24580
  29.6 6.0 %collective-permute-start.1 = (bf16[144,512]{1,0:T(8,128)(2,1)S(1)}, bf16[144,512]{1,0:T(8,128)(2,1)S(1)}, u32[]{:S(2)}, u32[]{:S(2)}) collective-permute-start(bf16[144,512]{1,0:T(8,128)(2,1)S(1)} %pad_maximum_fusion.2), channel_id=1, source_target_pairs={{0,7},{1,0},{2,1},{3,2},{4,3},{5,4},{6,5},{7,6},{8,15},{9,8},{10,9... | collective-permute-start | bytes 442376 | tf_op jit(solution)/shard_map/ppermute | solution.py:260
  32.9 30.2 %copy-start.1 = (bf16[2,512,2048]{2,1,0:T(8,128)(2,1)S(1)}, bf16[2,512,2048]{2,1,0:T(8,128)(2,1)}, u32[]{:S(2)}) copy-start(bf16[2,512,2048]{2,1,0:T(8,128)(2,1)} %wu_h.5) | copy-start | bytes 12582916
  32.9 30.2 %copy-start.5 = (bf16[2,512,512]{2,1,0:T(8,128)(2,1)S(1)}, bf16[2,512,512]{2,1,0:T(8,128)(2,1)}, u32[]{:S(2)}) copy-start(bf16[2,512,512]{2,1,0:T(8,128)(2,1)} %wo_h.5) | copy-start | bytes 3145732
  35.6 1.0 %copy-start.8 = (bf16[432,512]{1,0:T(8,128)(2,1)S(1)}, bf16[432,512]{1,0:T(8,128)(2,1)}, u32[]{:S(2)}) copy-start(bf16[432,512]{1,0:T(8,128)(2,1)} %copy-done.7) | copy-start | bytes 1327108
  36.6 1.0 %copy-start.10 = (bf16[432,512]{1,0:T(8,128)(2,1)S(1)}, bf16[432,512]{1,0:T(8,128)(2,1)}, u32[]{:S(2)}) copy-start(bf16[432,512]{1,0:T(8,128)(2,1)} %copy-done.9) | copy-start | bytes 1327108
  37.6 25.5 %copy-start.12 = (bf16[432,512]{1,0:T(8,128)(2,1)S(1)}, bf16[432,512]{1,0:T(8,128)(2,1)}, u32[]{:S(2)}) copy-start(bf16[432,512]{1,0:T(8,128)(2,1)} %copy-done.11) | copy-start | bytes 1327108
  37.6 25.5 %copy-start.14 = (bf16[432,512]{1,0:T(8,128)(2,1)S(1)}, bf16[432,512]{1,0:T(8,128)(2,1)}, u32[]{:S(2)}) copy-start(bf16[432,512]{1,0:T(8,128)(2,1)} %copy-done.13) | copy-start | bytes 1327108
  43.7 7.8 %collective-permute-start.2 = (bf16[144,512]{1,0:T(8,128)(2,1)S(1)}, bf16[144,512]{1,0:T(8,128)(2,1)S(1)}, u32[]{:S(2)}, u32[]{:S(2)}) collective-permute-start(bf16[144,512]{1,0:T(8,128)(2,1)S(1)} %pad_maximum_fusion.3), channel_id=1, source_target_pairs={{0,1},{1,2},{2,3},{3,4},{4,5},{5,6},{6,7},{7,0},{8,9},{9,10},{10,1... | collective-permute-start | bytes 442376 | tf_op jit(solution)/shard_map/ppermute | solution.py:260
  51.5 11.6 %collective-permute-start.3 = (bf16[432,512]{1,0:T(8,128)(2,1)S(1)}, bf16[432,512]{1,0:T(8,128)(2,1)S(1)}, u32[]{:S(2)}, u32[]{:S(2)}) collective-permute-start(bf16[432,512]{1,0:T(8,128)(2,1)S(1)} %pad_maximum_fusion), channel_id=1, source_target_pairs={{0,8},{8,16},{16,24},{24,32},{32,40},{40,48},{48,56},{56,64},{64,7... | collective-permute-start | bytes 1327112 | tf_op jit(solution)/shard_map/ppermute | solution.py:260
where the time goes:
time: 74 us; the launch traced here: 73.7 us
  Pallas kernels  30.6 us (41%)
  waiting for transfers between devices  20.7 us (28%)
  local copies, waits for them, and re-layouts  11.6 us (16%)
  starting transfers between devices  10.6 us (14%)
    ppermute x4, waiting for transfers between devices, ring(): lax.ppermute(value, axis, [(i, (i + by) % length) for i in range(length)])  20.7 us
    ppermute x4, starting transfers between devices, ring(): lax.ppermute(value, axis, [(i, (i + by) % length) for i in range(length)])  10.6 us
    unnamed x36, local copies, waits for them, and re-layouts  10.4 us
    pallas_call x1, Pallas kernels, call_first(): pl.pallas_call(first_kernel, out_shape=[half_shape()] * 4, in_specs=[VM,...  9.85 us
    pallas_call x1, Pallas kernels, call_fourth(): pl.pallas_call(fourth_kernel, out_shape=jax.ShapeDtypeStruct((216, 1024),...  9.48 us
    pallas_call x1, Pallas kernels, call_third(): pl.pallas_call(third_kernel, out_shape=[half_shape()] * 2, in_specs=[SM,...  5.97 us
    pallas_call x1, Pallas kernels, call_second(): pl.pallas_call(second_kernel, out_shape=[half_shape()] * 2, in_specs=[VM,...  5.28 us
  transfers between devices with their start and end apart: 4, of which 3 were waited for; matrix products, arithmetic and copies ran while one was open for 0% of the time, Pallas kernels for 7%

commit v1 on v0

v1 whole, which is shorter than its diff:
```python
import functools

import jax
import jax.numpy as jnp
from jax import lax
from jax.experimental import pallas as pl
from jax.experimental.pallas import tpu as pltpu
from jax.sharding import PartitionSpec as P

EPSILON = 1e-05
D = 512
FF = 2048
COLS, ROWS, LEV = 12, 18, 4
HALF = 432
ALL = 864
WIN = 144
F32 = jnp.float32
BF16 = jnp.bfloat16
VMEM_LIMIT = 20 * 1024 * 1024


def norm_rows(values, gain):
    center = jnp.mean(values, axis=-1, keepdims=True)
    off = values - center
    spread = jnp.mean(off * off, axis=-1, keepdims=True)
    return off * lax.rsqrt(spread + EPSILON) * gain


def round_bf16(values):
    return values.astype(BF16).astype(F32)


def mm(a, b):
    return jnp.dot(a, b, preferred_element_type=F32)


def gelu(x):
    inner = 0.7978845608028654 * (x + 0.044715 * (x * x * x))
    return 0.5 * x * (1.0 + jnp.tanh(inner))


def attend_unit(packed_ref, row0, count, group, mask):
    span = pl.ds(row0, WIN)
    lo = group * 256
    q = packed_ref[pl.ds(row0, count), lo : lo + 256] * jnp.asarray(0.125, BF16)
    k = packed_ref[span, D + lo : D + lo + 256]
    v = packed_ref[span, 2 * D + lo : 2 * D + lo + 256]
    lane = lax.broadcasted_iota(jnp.int32, (count, 256), 1) // 64
    zero = jnp.zeros_like(q)
    stacked = jnp.concatenate([jnp.where(lane == h, q, zero) for h in range(4)], axis=0)
    scores = lax.dot_general(stacked, k, (((1,), (1,)), ((), ())), preferred_element_type=F32)
    if mask is not None:
        scores = jnp.where(mask, scores, -1e30)
    e = jnp.exp(scores - jnp.max(scores, axis=1, keepdims=True))
    total = jnp.sum(e, axis=1, keepdims=True)
    mixed = mm(e.astype(BF16), v) * (1.0 / total)
    out = mixed[0:count]
    for h in range(1, 4):
        out = jnp.where(lane == h, mixed[h * count : (h + 1) * count], out)
    return out


def finish_rows(stream, attended, wo, wu, wd, gain):
    middle = round_bf16(stream + mm(attended, wo[...]))
    hidden_in = norm_rows(middle, gain).astype(BF16)
    total = middle
    for c in range(4):
        raised = mm(hidden_in, wu[:, c * 512 : (c + 1) * 512])
        total = total + mm(gelu(raised).astype(BF16), wd[c * 512 : (c + 1) * 512, :])
    return round_bf16(total)


def put_rows(ref, start, values):
    for j in range(4):
        ref[j, start : start + values.shape[0], :] = values[:, j * 128 : (j + 1) * 128]


def window_runs(base, levels, first_half):
    if first_half is None:
        return [(base + level, 72) for level in levels]
    return [(base + half * 144 + level, 36) for half in (first_half, 1 - first_half) for level in levels]


def gather_run(src, j, runs):
    return jnp.concatenate([src[j, pl.ds(start, count, stride=4), :] for start, count in runs], axis=0)


def scatter_run(dst, group, runs, out):
    at = 0
    for start, count in runs:
        for j in range(2):
            dst[group * 2 + j, pl.ds(start, count, stride=4), :] = out[at : at + count, j * 128 : (j + 1) * 128]
        at += count


def gather_windows(src, dst, windows):
    for w, runs in enumerate(windows):
        for j in range(4):
            dst[w * WIN : (w + 1) * WIN, j * 128 : (j + 1) * 128] = gather_run(src, j, runs).astype(BF16)


def project(nw, packed, wqkv):
    for c in range(6):
        packed[:, c * 256 : (c + 1) * 256] = mm(nw[...], wqkv[:, c * 256 : (c + 1) * 256]).astype(BF16)


def half_of(ref, which):
    pieces = [ref[j, 0:ALL, :].reshape(ROWS, 48, 128)[:, which * 24 : which * 24 + 24].reshape(HALF, 128) for j in range(4)]
    return jnp.concatenate(pieces, axis=1)


def load(sems, *pairs):
    groups, used = [], 0
    for source, target in pairs:
        rows = target.shape[0]
        parts = 4 if rows >= 512 else 1
        step = rows // parts
        group = []
        for i in range(parts):
            piece = (source.at[pl.ds(i * step, step)], target.at[pl.ds(i * step, step)]) if parts > 1 else (source, target)
            group.append(pltpu.make_async_copy(*piece, sems.at[used]))
            group[-1].start()
            used += 1
        groups.append(group)
    return groups


def wait(*groups):
    for group in groups:
        for copy in group:
            copy.wait()


def lanes(ref):
    return jnp.concatenate([ref[j] for j in range(4)], axis=1)


def take_stream(x, dst, at, rows):
    for r in range(rows):
        for p in range(6):
            pair = jnp.concatenate([x[2 * p, r].astype(F32), x[2 * p + 1, r].astype(F32)], axis=0)
            put_rows(dst, at + r * 48 + p * 8, pair)


PLAIN = [window_runs(i * 288, levels, None) for levels in ((0, 1), (2, 3)) for i in range(3)]


def first_kernel(x_h, wqkv_h, wo_h, wu_h, wd_h, gains_h, first_a, normed_a, x_b, att_b, wo, wu, wd, gains,
                 x, xs, ns, nw, packed, wqkv, sems):
    copies = load(sems, (x_h, x), (gains_h, gains), (wqkv_h.at[0], wqkv), (wo_h.at[0], wo), (wu_h.at[0], wu),
                  (wd_h.at[0], wd))
    wait(*copies[:2])
    take_stream(x, xs, 0, ROWS)
    put_rows(ns, 0, norm_rows(lanes(xs), gains[0, 0:1]))
    gather_windows(ns, nw, PLAIN)
    wait(copies[2])
    project(nw, packed, wqkv)
    for w, runs in enumerate(PLAIN):
        for group in range(2):
            scatter_run(ns, group, runs, attend_unit(packed, w * WIN, WIN, group, None))
    x_b[...] = half_of(xs, 1).astype(BF16)
    att_b[...] = half_of(ns, 1).astype(BF16)
    wait(*copies[3:])
    result = finish_rows(half_of(xs, 0), half_of(ns, 0).astype(BF16), wo, wu, wd, gains[0, 1:2])
    first_a[...] = result.astype(BF16)
    normed_a[...] = norm_rows(result, gains[1, 0:1]).astype(BF16)


BESIDE = [window_runs(side * 288, levels, 1 - side) for levels in ((0, 1), (2, 3)) for side in range(2)]


def halo_kernel(before, after, wqkv_h, wo, wu, wd, gains, halo_a, halo_b, xs, ns, nw, packed, wqkv, sems):
    copies = load(sems, (wqkv_h.at[0], wqkv))
    take_stream(before, xs, 0, 6)
    take_stream(after, xs, 288, 6)
    put_rows(ns, 0, norm_rows(lanes(xs), gains[0, 0:1]))
    gather_windows(ns, nw, BESIDE)
    wait(*copies)
    project(nw, packed, wqkv)
    attended, stream = [], []
    for w, runs in enumerate(BESIDE):
        parts = [attend_unit(packed, w * WIN, 72, group, None) for group in range(2)]
        attended.append(jnp.concatenate(parts, axis=1))
        stream.append(jnp.concatenate([gather_run(xs, j, runs[:2]) for j in range(4)], axis=1))
    result = finish_rows(jnp.concatenate(stream, axis=0), jnp.concatenate(attended, axis=0).astype(BF16),
                         wo, wu, wd, gains[0, 1:2])
    result = norm_rows(result, gains[1, 0:1])
    for w, runs in enumerate(BESIDE):
        for group in range(2):
            scatter_run(ns, group, runs[:2], result[w * 72 : w * 72 + 72, group * 256 : group * 256 + 256])
    near = jnp.concatenate([lanes(ns)[144:288], lanes(ns)[288:432]], axis=0).reshape(6, 48, D)
    halo_a[...] = near[:, 0:24].reshape(144, D).astype(BF16)
    halo_b[...] = near[:, 24:48].reshape(144, D).astype(BF16)


def second_kernel(x_b, att_b, wo, wu, wd, gains, first_b, normed_b):
    result = finish_rows(x_b[...].astype(F32), att_b[...], wo, wu, wd, gains[0, 1:2])
    first_b[...] = result.astype(BF16)
    normed_b[...] = norm_rows(result, gains[1, 0:1]).astype(BF16)


HALVES = (1, None, None, 0)
SHIFTED = [window_runs(i * 288, levels, HALVES[i]) for levels in ((1, 2), (3, 0)) for i in range(4)]


def third_kernel(edge, n_b, n_ra, halo_b, halo_ra, wqkv_h, wo_h, wu_h, wd_h, z_b, z_ra, wo, wu, wd,
                 ns, nw, packed, wqkv, sems):
    copies = load(sems, (wqkv_h.at[1], wqkv), (wo_h.at[1], wo), (wu_h.at[1], wu), (wd_h.at[1], wd))
    for which, (ref, halo) in enumerate(((n_b, halo_b), (n_ra, halo_ra))):
        rows = ref[...].astype(F32).reshape(ROWS, 24, D)
        extra = halo[...].astype(F32).reshape(6, 24, D)
        for r in range(24):
            put_rows(ns, r * 48 + which * 24, rows[r - 3] if 3 <= r < 21 else extra[r if r < 3 else r - 18])
    gather_windows(ns, nw, SHIFTED)
    wait(copies[0])
    project(nw, packed, wqkv)
    for w, runs in enumerate(SHIFTED):
        i, lonely = w % 4, w >= 4
        count = WIN if HALVES[i] is None else 72
        key = lax.broadcasted_iota(jnp.int32, (4 * count, WIN), 1)
        query = lax.rem(lax.broadcasted_iota(jnp.int32, (4 * count, WIN), 0), count)
        mask = None
        if lonely:
            mask = (lax.rem(key, count) < count // 2) == (query < count // 2)
        if count == 72:
            inside = (key < 72) | (edge[i // 3] == 0)
            mask = inside if mask is None else mask & inside
            runs = runs[:2]
        runs = [(start - 144, length) for start, length in runs]
        for group in range(2):
            scatter_run(ns, group, runs, attend_unit(packed, w * WIN, count, group, mask))
    z_b[...] = half_of(ns, 0).astype(BF16)
    z_ra[...] = half_of(ns, 1).astype(BF16)
    wait(*copies[1:])


def fourth_kernel(f_b, att_b, wo, wu, wd, gains, second_b):
    second_b[...] = finish_rows(f_b[...].astype(F32), att_b[...], wo, wu, wd, gains[1, 1:2]).astype(BF16)


def fifth_kernel(f_a, att_a, second_b, wo, wu, wd, gains, mg_h, wm_h, out, merge_gain, wm, sems):
    copies = load(sems, (mg_h, merge_gain), (wm_h, wm))
    s_a = finish_rows(f_a[...].astype(F32), att_a[...], wo, wu, wd, gains[1, 1:2]).reshape(9, 2, 3, 8, D)
    s_b = second_b[...].astype(F32).reshape(9, 2, 3, 8, D)
    top = lax.broadcasted_iota(jnp.int32, (216, D), 0) % 8 < 4
    parts = []
    for rp in range(2):
        a = s_a[:, rp].reshape(216, D)
        b = s_b[:, rp].reshape(216, D)
        a_turned = pltpu.roll(a.reshape(27, 8, D), 4, 1).reshape(216, D)
        b_turned = pltpu.roll(b.reshape(27, 8, D), 4, 1).reshape(216, D)
        parts.append(jnp.where(top, a, b_turned))
        parts.append(jnp.where(top, a_turned, b))
    center = sum(jnp.sum(p, axis=-1, keepdims=True) for p in parts) * (1.0 / 2048)
    parts = [p - center for p in parts]
    spread = sum(jnp.sum(p * p, axis=-1, keepdims=True) for p in parts) * (1.0 / 2048)
    scale = lax.rsqrt(spread + EPSILON)
    wait(copies[0])
    total = None
    for i, p in enumerate(parts):
        copies[1][i].wait()
        normed = (p * scale * merge_gain[0:1, i * 512 : (i + 1) * 512]).astype(BF16)
        term = mm(normed, wm[i * 512 : (i + 1) * 512, :])
        total = term if total is None else total + term
    for j in range(9):
        for i in range(3):
            at = (j * 3 + i) * 8
            out[i, j] = total[at : at + 4].astype(BF16)
            out[3 + i, j] = total[at + 4 : at + 8].astype(BF16)


VM = pl.BlockSpec(memory_space=pltpu.VMEM)


def half(count):
    return [pltpu.VMEM((HALF, D), BF16)] * count


def rows_f32(tokens):
    return pltpu.VMEM((4, tokens, 128), F32)


def attention_scratch(tokens):
    return [rows_f32(tokens), pltpu.VMEM((tokens, D), BF16), pltpu.VMEM((tokens, 3 * D), BF16)]


QKV = [pltpu.VMEM((D, 3 * D), BF16)]
FINISH = [pltpu.VMEM((D, D), BF16), pltpu.VMEM((D, FF), BF16), pltpu.VMEM((FF, D), BF16)]
GAINS = [pltpu.VMEM((2, 2, D), F32)]
MERGE = [pltpu.VMEM((1, 4 * D), F32), pltpu.VMEM((4 * D, 1024), BF16)]


def call(kernel, name, outs, args, scratch, sems, flops):
    values = [pltpu.with_memory_space_constraint(v, pltpu.HBM) if m is pltpu.HBM else v for v, m in args]
    outs = [jax.ShapeDtypeStruct(o.shape, o.dtype) for o in outs]
    return pl.pallas_call(
        kernel,
        out_shape=outs,
        in_specs=[pl.BlockSpec(memory_space=m) for _, m in args],
        out_specs=jax.tree.map(lambda _: VM, outs),
        scratch_shapes=scratch + ([pltpu.SemaphoreType.DMA((4 * sems,))] if sems else []),
        compiler_params=pltpu.CompilerParams(vmem_limit_bytes=VMEM_LIMIT),
        cost_estimate=pl.CostEstimate(flops=flops, bytes_accessed=6_000_000, transcendentals=900_000),
        name=name,
    )(*values)


def hbm(*values):
    return [(v, pltpu.HBM) for v in values]


def vmem(*values):
    return [(v, pltpu.VMEM) for v in values]


def ring(value, axis, by):
    length = lax.axis_size(axis)
    return lax.ppermute(value, axis, [(i, (i + by) % length) for i in range(length)])


def body(stream, w_qkv, w_out, w_up, w_down, gains, merge_gain, w_merge):
    place = lax.axis_index("lat")
    edge = jnp.stack([place == 0, place == lax.axis_size("lat") - 1]).astype(jnp.int32)
    after = ring(stream[:, :6], "lat", -1)
    before = ring(stream[:, 12:], "lat", 1)
    first_a, normed_a, x_b, att_b, wo0, wu0, wd0, gains = call(
        first_kernel, "block_one", half(4) + FINISH + GAINS, hbm(stream, w_qkv, w_out, w_up, w_down, gains),
        [pltpu.VMEM((COLS, ROWS, LEV, D), BF16), rows_f32(ALL)] + attention_scratch(ALL) + QKV, 6, 6_000_000_000)
    normed_ra = ring(normed_a, "lon", -1)
    halo_a, halo_b = call(
        halo_kernel, "block_one_beside", [pltpu.VMEM((144, D), BF16)] * 2,
        vmem(before, after) + hbm(w_qkv) + vmem(wo0, wu0, wd0, gains),
        [rows_f32(576)] + attention_scratch(576) + QKV, 1, 4_000_000_000)
    halo_ra = ring(halo_a, "lon", -1)
    first_b, normed_b = call(
        second_kernel, "block_one_rest", half(2), vmem(x_b, att_b, wo0, wu0, wd0, gains), [], 0, 4_000_000_000)
    z_b, z_ra, wo1, wu1, wd1 = call(
        third_kernel, "shifted_attention", half(2) + FINISH,
        [(edge, pltpu.SMEM)] + vmem(normed_b, normed_ra, halo_b, halo_ra) + hbm(w_qkv, w_out, w_up, w_down),
        attention_scratch(1152) + QKV, 4, 4_000_000_000)
    att_a = ring(z_ra, "lon", 1)
    second_b, = call(
        fourth_kernel, "block_two_rest", half(1), vmem(first_b, z_b, wo1, wu1, wd1, gains), [], 0, 4_000_000_000)
    out, = call(
        fifth_kernel, "merge", [jax.ShapeDtypeStruct((6, 9, LEV, 1024), BF16)],
        vmem(first_a, att_a, second_b, wo1, wu1, wd1, gains) + hbm(merge_gain.reshape(1, -1), w_merge),
        MERGE, 2, 5_000_000_000)
    return out


def solution(mesh):
    return jax.shard_map(
        body,
        mesh=mesh,
        in_specs=(P("lon", "lat", None, None), P(), P(), P(), P(), P(), P(), P()),
        out_specs=P("lon", "lat", None, None),
        check_vma=False,
    )
```

time: 74 us -> 59.6 us (0.81)
  waiting for transfers between devices: 20.7 us -> 8.18 us
  local copies, waits for them, and re-layouts: 11.6 us -> 1.26 us
  Pallas kernels: 30.6 us -> 36.2 us
  starting transfers between devices: 10.6 us -> 13.6 us
    ppermute x4 -> x5, waiting for transfers between devices: 20.7 us -> 8.18 us  [ring(): lax.ppermute(value, axis, [(i, (i + by) % length) for i in range(length)])]
    unnamed x36 -> x0, local copies, waits for them, and re-layouts: 10.4 us -> none
    pallas_call x4 -> x6, Pallas kernels: 30.6 us -> 36.2 us  [call(): pl.pallas_call(kernel, out_shape=outs, in_specs=[pl.BlockSpec(memory_spac...]
    ppermute x4 -> x5, starting transfers between devices: 10.6 us -> 13.6 us  [ring(): lax.ppermute(value, axis, [(i, (i + by) % length) for i in range(length)])]
    slice x7 -> x1, local copies, waits for them, and re-layouts: 0.09 us -> 1.26 us  [body(): after = ring(stream[:, :6], 'lat', -1)]
    transpose x1 -> x0, local copies, waits for them, and re-layouts: 0.92 us -> none  [body(): out = out.reshape(9, 3, 2, LEV, 1024).transpose(2, 1, 0, 3, 4)]
  transfers between devices with their start and end apart: 4 -> 5, of which waited for: 3 -> 1; matrix products, arithmetic and copies ran while one was open for 0% -> 0% of each run, Pallas kernels for 7% -> 37%
where the time goes in v1:
time: 59.6 us; the launch traced here: 59.5 us
  Pallas kernels  36.2 us (61%)
  starting transfers between devices  13.6 us (23%)
  waiting for transfers between devices  8.18 us (14%)
  local copies, waits for them, and re-layouts  1.26 us (2%)
    pallas_call x6, Pallas kernels, call(): pl.pallas_call(kernel, out_shape=outs, in_specs=[pl.BlockSpec(memory_spac...  36.2 us
    ppermute x5, starting transfers between devices, ring(): lax.ppermute(value, axis, [(i, (i + by) % length) for i in range(length)])  13.6 us
    ppermute x5, waiting for transfers between devices, ring(): lax.ppermute(value, axis, [(i, (i + by) % length) for i in range(length)])  8.18 us
    slice x1, local copies, waits for them, and re-layouts, body(): after = ring(stream[:, :6], 'lat', -1)  1.26 us
  transfers between devices with their start and end apart: 5, of which 1 were waited for; matrix products, arithmetic and copies ran while one was open for 0% of the time, Pallas kernels for 37%

profile of v1, /device:TPU:0, one launch (start us, length us, event | category | flops | bytes accessed | tf_op | source)
XLA Modules:
  0.0 59.5 jit_solution(11725214958616131387)
XLA Ops:
  0.0 1.3 %fusion = (bf16[12,6,4,512]{3,2,1,0:T(4,128)(2,1)S(1)}, bf16[12,6,4,512]{3,2,1,0:T(4,128)(2,1)S(1)}) fusion(bf16[12,18,4,512]{3,2,1,0:T(4,128)(2,1)} %x_h.1), kind=kLoop, calls=%fused_computation.1 | loop fusion | bytes 1179648 | tf_op jit(solution)/shard_map/slice | solution.py:324
  1.3 4.1 %collective-permute-start.2 = (bf16[12,6,4,512]{3,2,1,0:T(4,128)(2,1)S(1)}, bf16[12,6,4,512]{3,2,1,0:T(4,128)(2,1)S(1)}, u32[]{:S(2)}, u32[]{:S(2)}) collective-permute-start(bf16[12,6,4,512]{3,2,1,0:T(4,128)(2,1)S(1)} %get-tuple-element.39), channel_id=1, source_target_pairs={{0,7},{1,0},{2,1},{3,2},{4,3},{5,4},{6,5},{7,6},{8,15},{9,8},{10,9... | collective-permute-start | bytes 884744 | tf_op jit(solution)/shard_map/ppermute | solution.py:318
  5.4 0.0 collective-permute-start.1
  5.4 9.5 %block_one.1 = (bf16[432,512]{1,0:T(8,128)(2,1)S(1)}, bf16[432,512]{1,0:T(8,128)(2,1)S(1)}, bf16[432,512]{1,0:T(8,128)(2,1)S(1)}, bf16[432,512]{1,0:T(8,128)(2,1...) custom-call(bf16[12,18,4,512]{3,2,1,0:T(4,128)(2,1)} %x_h.1, ...), custom_call_target="tpu_custom_call" | custom-call | flops 6000000000 | bytes 6000000 | tf_op jit(solution)/shard_map/block_one/pallas_call | solution.py:296
  14.9 5.6 %collective-permute-start = (bf16[432,512]{1,0:T(8,128)(2,1)S(1)}, bf16[432,512]{1,0:T(8,128)(2,1)S(1)}, u32[]{:S(2)}, u32[]{:S(2)}) collective-permute-start(bf16[432,512]{1,0:T(8,128)(2,1)S(1)} %get-tuple-element.30), channel_id=1, source_target_pairs={{0,120},{8,0},{16,8},{24,16},{32,24},{40,32},{48,40},{56,48},{64,5... | collective-permute-start | bytes 1327112 | tf_op jit(solution)/shard_map/ppermute | solution.py:318
  20.5 0.0 collective-permute-done.2.after
  20.5 0.0 collective-permute-done.1.before
  20.5 6.0 %block_one_beside.1 = (bf16[144,512]{1,0:T(8,128)(2,1)S(1)}, bf16[144,512]{1,0:T(8,128)(2,1)S(1)}) custom-call(bf16[12,6,4,512]{3,2,1,0:T(4,128)(2,1)S(1)} %collective-permute-done.1.before, bf16[12,6,4,512]{3,2,1,0:T(4,128)(2,1)S(1)} %collective-permute-done.2.after, bf16[2,512,1536]{2,1,0:T(8,128)(2,1)} %wqkv_h.5, ...), custom_call_target="tpu_custom_call" | custom-call | flops 4000000000 | bytes 6000000 | tf_op jit(solution)/shard_map/block_one_beside/pallas_call | solution.py:296
  26.5 3.6 %collective-permute-start.3 = (bf16[144,512]{1,0:T(8,128)(2,1)S(1)}, bf16[144,512]{1,0:T(8,128)(2,1)S(1)}, u32[]{:S(2)}, u32[]{:S(2)}) collective-permute-start(bf16[144,512]{1,0:T(8,128)(2,1)S(1)} %get-tuple-element.32), channel_id=1, source_target_pairs={{0,120},{8,0},{16,8},{24,16},{32,24},{40,32},{48,40},{56,48},{64,5... | collective-permute-start | bytes 442376 | tf_op jit(solution)/shard_map/ppermute | solution.py:318
  30.1 3.4 %block_one_rest.1 = (bf16[432,512]{1,0:T(8,128)(2,1)S(1)}, bf16[432,512]{1,0:T(8,128)(2,1)S(1)}) custom-call(bf16[432,512]{1,0:T(8,128)(2,1)S(1)} %get-tuple-element.23.x_b, bf16[432,512]{1,0:T(8,128)(2,1)S(1)} %get-tuple-element.24.att_b, bf16[512,512]{1,0:T(8,128)(2,1)S(1)} %get-tuple-element.25.wo, bf16[512,2048]{1,0:T(8,128)(2,1)S(1)} %get-tuple-element.26.wu, ...), custom_call_target="tpu_custom_call" | custom-call | flops 4000000000 | bytes 6000000 | tf_op jit(solution)/shard_map/block_one_rest/pallas_call | solution.py:296
  33.5 0.1 add_convert_fusion.edge
  33.5 0.0 collective-permute-done.3.halo_ra
  33.5 0.0 collective-permute-done.n_ra
  33.5 7.1 %shifted_attention.1 = (bf16[432,512]{1,0:T(8,128)(2,1)S(1)}, bf16[432,512]{1,0:T(8,128)(2,1)S(1)}, bf16[512,512]{1,0:T(8,128)(2,1)S(1)}, bf16[512,2048]{1,0:T(8,128)(2,1)S(1)}, bf16[2048,512]{1,0:T(8,128)(2,1)S(1)}) custom-call(s32[2]{0:T(128)S(1)} %add_convert_fusion.edge, bf16[432,512]{1,0:T(8,128)(2,1)S(1)} %get-tuple-element.29.n_b, ...), custom_call_target="tpu_custom_call" | custom-call | flops 4000000000 | bytes 6000000 | tf_op jit(solution)/shard_map/shifted_attention/pallas_call | solution.py:296
  40.6 0.3 collective-permute-start.4
  41.0 3.2 %block_two_rest.1.second_b = bf16[432,512]{1,0:T(8,128)(2,1)S(1)} custom-call(bf16[432,512]{1,0:T(8,128)(2,1)S(1)} %get-tuple-element.34.f_b, bf16[432,512]{1,0:T(8,128)(2,1)S(1)} %get-tuple-element.35.att_b, bf16[512,512]{1,0:T(8,128)(2,1)S(1)} %get-tuple-element.36.wo, bf16[512,2048]{1,0:T(8,128)(2,1)S(1)} %get-tuple-element.37.wu, ...), custom_call_target="tpu_custom_call" | custom-call | flops 4000000000 | bytes 6000000 | tf_op jit(solution)/shard_map/block_two_rest/pallas_call | solution.py:296
  44.1 8.2 %collective-permute-done.4.att_a = bf16[432,512]{1,0:T(8,128)(2,1)S(1)} collective-permute-done((bf16[432,512]{1,0:T(8,128)(2,1)S(1)}, bf16[432,512]{1,0:T(8,128)(2,1)S(1)}, u32[]{:S(2)}, u32[]{:S(2)}) %collective-permute-start.4) | collective-permute-done | bytes 442400 | tf_op jit(solution)/shard_map/ppermute | solution.py:318
  52.3 7.0 %merge.1 = bf16[6,9,4,1024]{3,2,1,0:T(4,128)(2,1)} custom-call(bf16[432,512]{1,0:T(8,128)(2,1)S(1)} %get-tuple-element.22.f_a, bf16[432,512]{1,0:T(8,128)(2,1)S(1)} %collective-permute-done.4.att_a, bf16[432,512]{1,0:T(8,128)(2,1)S(1)} %block_two_rest.1.second_b, bf16[512,512]{1,0:T(8,128)(2,1)S(1)} %get-tuple-element.36.wo, ...), custom_call_target="tpu_custom_call" | custom-call | flops 5000000000 | bytes 6000000 | tf_op jit(solution)/shard_map/merge/pallas_call | solution.py:296
Async XLA Ops:
  1.3 19.2 %collective-permute-start.2 = (bf16[12,6,4,512]{3,2,1,0:T(4,128)(2,1)S(1)}, bf16[12,6,4,512]{3,2,1,0:T(4,128)(2,1)S(1)}, u32[]{:S(2)}, u32[]{:S(2)}) collective-permute-start(bf16[12,6,4,512]{3,2,1,0:T(4,128)(2,1)S(1)} %get-tuple-element.39), channel_id=1, source_target_pairs={{0,7},{1,0},{2,1},{3,2},{4,3},{5,4},{6,5},{7,6},{8,15},{9,8},{10,9... | collective-permute-start | bytes 884744 | tf_op jit(solution)/shard_map/ppermute | solution.py:318
  5.4 15.1 %collective-permute-start.1 = (bf16[12,6,4,512]{3,2,1,0:T(4,128)(2,1)S(1)}, bf16[12,6,4,512]{3,2,1,0:T(4,128)(2,1)S(1)}, u32[]{:S(2)}, u32[]{:S(2)}) collective-permute-start(bf16[12,6,4,512]{3,2,1,0:T(4,128)(2,1)S(1)} %get-tuple-element.40), channel_id=1, source_target_pairs={{0,1},{1,2},{2,3},{3,4},{4,5},{5,6},{6,7},{7,0},{8,9},{9,10},{10,1... | collective-permute-start | bytes 884744 | tf_op jit(solution)/shard_map/ppermute | solution.py:318
  14.9 18.7 %collective-permute-start = (bf16[432,512]{1,0:T(8,128)(2,1)S(1)}, bf16[432,512]{1,0:T(8,128)(2,1)S(1)}, u32[]{:S(2)}, u32[]{:S(2)}) collective-permute-start(bf16[432,512]{1,0:T(8,128)(2,1)S(1)} %get-tuple-element.30), channel_id=1, source_target_pairs={{0,120},{8,0},{16,8},{24,16},{32,24},{40,32},{48,40},{56,48},{64,5... | collective-permute-start | bytes 1327112 | tf_op jit(solution)/shard_map/ppermute | solution.py:318
  26.5 7.0 %collective-permute-start.3 = (bf16[144,512]{1,0:T(8,128)(2,1)S(1)}, bf16[144,512]{1,0:T(8,128)(2,1)S(1)}, u32[]{:S(2)}, u32[]{:S(2)}) collective-permute-start(bf16[144,512]{1,0:T(8,128)(2,1)S(1)} %get-tuple-element.32), channel_id=1, source_target_pairs={{0,120},{8,0},{16,8},{24,16},{32,24},{40,32},{48,40},{56,48},{64,5... | collective-permute-start | bytes 442376 | tf_op jit(solution)/shard_map/ppermute | solution.py:318
  40.6 11.6 %collective-permute-start.4 = (bf16[432,512]{1,0:T(8,128)(2,1)S(1)}, bf16[432,512]{1,0:T(8,128)(2,1)S(1)}, u32[]{:S(2)}, u32[]{:S(2)}) collective-permute-start(bf16[432,512]{1,0:T(8,128)(2,1)S(1)} %get-tuple-element.33), channel_id=1, source_target_pairs={{0,8},{8,16},{16,24},{24,32},{32,40},{40,48},{48,56},{56,64},{64,7... | collective-permute-start | bytes 1327112 | tf_op jit(solution)/shard_map/ppermute | solution.py:318

commit v2 on v1

--- a/solution.py
+++ b/solution.py
@@ -145,22 +145,22 @@
 PLAIN = [window_runs(i * 288, levels, None) for levels in ((0, 1), (2, 3)) for i in range(3)]
 
 
-def first_kernel(x_h, wqkv_h, wo_h, wu_h, wd_h, gains_h, first_a, normed_a, x_b, att_b, wo, wu, wd, gains,
-                 x, xs, ns, nw, packed, wqkv, sems):
-    copies = load(sems, (x_h, x), (gains_h, gains), (wqkv_h.at[0], wqkv), (wo_h.at[0], wo), (wu_h.at[0], wu),
-                  (wd_h.at[0], wd))
-    wait(*copies[:2])
+def first_kernel(x_h, wqkv_h, wo_h, wu_h, wd_h, gains_h, first_a, normed_a, x_b, att_b, wqkv, wo, wu, wd, gains,
+                 x, xs, ns, nw, packed, sems):
+    early = load(sems, (x_h, x), (gains_h, gains), (wqkv_h.at[0], wqkv))
+    wait(*early[:2])
     take_stream(x, xs, 0, ROWS)
     put_rows(ns, 0, norm_rows(lanes(xs), gains[0, 0:1]))
     gather_windows(ns, nw, PLAIN)
-    wait(copies[2])
+    wait(early[2])
+    copies = load(sems.at[6:], (wo_h.at[0], wo), (wu_h.at[0], wu), (wd_h.at[0], wd))
     project(nw, packed, wqkv)
     for w, runs in enumerate(PLAIN):
         for group in range(2):
             scatter_run(ns, group, runs, attend_unit(packed, w * WIN, WIN, group, None))
     x_b[...] = half_of(xs, 1).astype(BF16)
     att_b[...] = half_of(ns, 1).astype(BF16)
-    wait(*copies[3:])
+    wait(*copies)
     result = finish_rows(half_of(xs, 0), half_of(ns, 0).astype(BF16), wo, wu, wd, gains[0, 1:2])
     first_a[...] = result.astype(BF16)
     normed_a[...] = norm_rows(result, gains[1, 0:1]).astype(BF16)
@@ -169,13 +169,11 @@
 BESIDE = [window_runs(side * 288, levels, 1 - side) for levels in ((0, 1), (2, 3)) for side in range(2)]
 
 
-def halo_kernel(before, after, wqkv_h, wo, wu, wd, gains, halo_a, halo_b, xs, ns, nw, packed, wqkv, sems):
-    copies = load(sems, (wqkv_h.at[0], wqkv))
+def halo_kernel(before, after, wqkv, wo, wu, wd, gains, halo_a, halo_b, xs, ns, nw, packed):
     take_stream(before, xs, 0, 6)
     take_stream(after, xs, 288, 6)
     put_rows(ns, 0, norm_rows(lanes(xs), gains[0, 0:1]))
     gather_windows(ns, nw, BESIDE)
-    wait(*copies)
     project(nw, packed, wqkv)
     attended, stream = [], []
     for w, runs in enumerate(BESIDE):
@@ -205,14 +203,15 @@
 
 def third_kernel(edge, n_b, n_ra, halo_b, halo_ra, wqkv_h, wo_h, wu_h, wd_h, z_b, z_ra, wo, wu, wd,
                  ns, nw, packed, wqkv, sems):
-    copies = load(sems, (wqkv_h.at[1], wqkv), (wo_h.at[1], wo), (wu_h.at[1], wu), (wd_h.at[1], wd))
+    early = load(sems, (wqkv_h.at[1], wqkv))
     for which, (ref, halo) in enumerate(((n_b, halo_b), (n_ra, halo_ra))):
         rows = ref[...].astype(F32).reshape(ROWS, 24, D)
         extra = halo[...].astype(F32).reshape(6, 24, D)
         for r in range(24):
             put_rows(ns, r * 48 + which * 24, rows[r - 3] if 3 <= r < 21 else extra[r if r < 3 else r - 18])
+    copies = load(sems.at[4:], (wo_h.at[1], wo), (wu_h.at[1], wu), (wd_h.at[1], wd))
     gather_windows(ns, nw, SHIFTED)
-    wait(copies[0])
+    wait(*early)
     project(nw, packed, wqkv)
     for w, runs in enumerate(SHIFTED):
         i, lonely = w % 4, w >= 4
@@ -231,42 +230,49 @@
             scatter_run(ns, group, runs, attend_unit(packed, w * WIN, count, group, mask))
     z_b[...] = half_of(ns, 0).astype(BF16)
     z_ra[...] = half_of(ns, 1).astype(BF16)
-    wait(*copies[1:])
-
-
-def fourth_kernel(f_b, att_b, wo, wu, wd, gains, second_b):
-    second_b[...] = finish_rows(f_b[...].astype(F32), att_b[...], wo, wu, wd, gains[1, 1:2]).astype(BF16)
-
-
-def fifth_kernel(f_a, att_a, second_b, wo, wu, wd, gains, mg_h, wm_h, out, merge_gain, wm, sems):
-    copies = load(sems, (mg_h, merge_gain), (wm_h, wm))
-    s_a = finish_rows(f_a[...].astype(F32), att_a[...], wo, wu, wd, gains[1, 1:2]).reshape(9, 2, 3, 8, D)
-    s_b = second_b[...].astype(F32).reshape(9, 2, 3, 8, D)
-    top = lax.broadcasted_iota(jnp.int32, (216, D), 0) % 8 < 4
+    wait(*copies)
+
+
+def merge_half(values, gain, wm, landed, out):
+    pairs = values[: 8 * 48].reshape(4, 2, 2, 3, 8, D)
+    last = values[8 * 48 :].reshape(1, 2, 3, 8, D)
+    top = lax.broadcasted_iota(jnp.int32, (120, D), 0) % 8 < 4
     parts = []
     for rp in range(2):
-        a = s_a[:, rp].reshape(216, D)
-        b = s_b[:, rp].reshape(216, D)
-        a_turned = pltpu.roll(a.reshape(27, 8, D), 4, 1).reshape(216, D)
-        b_turned = pltpu.roll(b.reshape(27, 8, D), 4, 1).reshape(216, D)
-        parts.append(jnp.where(top, a, b_turned))
-        parts.append(jnp.where(top, a_turned, b))
+        even = jnp.concatenate([pairs[:, 0, rp], last[:, rp]], axis=0).reshape(15, 8, D)
+        odd = jnp.concatenate([pairs[:, 1, rp], last[:, rp]], axis=0).reshape(15, 8, D)
+        even_turned = pltpu.roll(even, 4, 1).reshape(120, D)
+        odd_turned = pltpu.roll(odd, 4, 1).reshape(120, D)
+        parts.append(jnp.where(top, even.reshape(120, D), odd_turned))
+        parts.append(jnp.where(top, even_turned, odd.reshape(120, D)))
     center = sum(jnp.sum(p, axis=-1, keepdims=True) for p in parts) * (1.0 / 2048)
     parts = [p - center for p in parts]
     spread = sum(jnp.sum(p * p, axis=-1, keepdims=True) for p in parts) * (1.0 / 2048)
     scale = lax.rsqrt(spread + EPSILON)
-    wait(copies[0])
     total = None
     for i, p in enumerate(parts):
-        copies[1][i].wait()
-        normed = (p * scale * merge_gain[0:1, i * 512 : (i + 1) * 512]).astype(BF16)
+        normed = (p * scale * gain[0:1, i * 512 : (i + 1) * 512]).astype(BF16)
+        landed(i)
         term = mm(normed, wm[i * 512 : (i + 1) * 512, :])
         total = term if total is None else total + term
     for j in range(9):
         for i in range(3):
-            at = (j * 3 + i) * 8
+            at = (j // 2 * 3 + i) * 8 + j % 2 * 4
             out[i, j] = total[at : at + 4].astype(BF16)
-            out[3 + i, j] = total[at + 4 : at + 8].astype(BF16)
+
+
+def fourth_kernel(f_b, att_b, wo, wu, wd, gains, mg_h, wm_h, out_b, gain, wm, sems):
+    copies = load(sems, (mg_h, gain), (wm_h, wm))
+    second = finish_rows(f_b[...].astype(F32), att_b[...], wo, wu, wd, gains[1, 1:2])
+    wait(copies[0])
+    merge_half(second, gain, wm, lambda i: copies[1][i].wait(), out_b)
+
+
+def fifth_kernel(f_a, att_a, out_b, wo, wu, wd, gains, gain, wm, out):
+    second = finish_rows(f_a[...].astype(F32), att_a[...], wo, wu, wd, gains[1, 1:2])
+    merge_half(second, gain, wm, lambda i: None, out)
+    for i in range(3):
+        out[3 + i] = out_b[i]
 
 
 VM = pl.BlockSpec(memory_space=pltpu.VMEM)
@@ -323,14 +329,13 @@
     edge = jnp.stack([place == 0, place == lax.axis_size("lat") - 1]).astype(jnp.int32)
     after = ring(stream[:, :6], "lat", -1)
     before = ring(stream[:, 12:], "lat", 1)
-    first_a, normed_a, x_b, att_b, wo0, wu0, wd0, gains = call(
-        first_kernel, "block_one", half(4) + FINISH + GAINS, hbm(stream, w_qkv, w_out, w_up, w_down, gains),
-        [pltpu.VMEM((COLS, ROWS, LEV, D), BF16), rows_f32(ALL)] + attention_scratch(ALL) + QKV, 6, 6_000_000_000)
+    first_a, normed_a, x_b, att_b, wqkv0, wo0, wu0, wd0, gains = call(
+        first_kernel, "block_one", half(4) + QKV + FINISH + GAINS, hbm(stream, w_qkv, w_out, w_up, w_down, gains),
+        [pltpu.VMEM((COLS, ROWS, LEV, D), BF16), rows_f32(ALL)] + attention_scratch(ALL), 6, 6_000_000_000)
     normed_ra = ring(normed_a, "lon", -1)
     halo_a, halo_b = call(
         halo_kernel, "block_one_beside", [pltpu.VMEM((144, D), BF16)] * 2,
-        vmem(before, after) + hbm(w_qkv) + vmem(wo0, wu0, wd0, gains),
-        [rows_f32(576)] + attention_scratch(576) + QKV, 1, 4_000_000_000)
+        vmem(before, after, wqkv0, wo0, wu0, wd0, gains), [rows_f32(576)] + attention_scratch(576), 0, 4_000_000_000)
     halo_ra = ring(halo_a, "lon", -1)
     first_b, normed_b = call(
         second_kernel, "block_one_rest", half(2), vmem(x_b, att_b, wo0, wu0, wd0, gains), [], 0, 4_000_000_000)
@@ -339,12 +344,12 @@
         [(edge, pltpu.SMEM)] + vmem(normed_b, normed_ra, halo_b, halo_ra) + hbm(w_qkv, w_out, w_up, w_down),
         attention_scratch(1152) + QKV, 4, 4_000_000_000)
     att_a = ring(z_ra, "lon", 1)
-    second_b, = call(
-        fourth_kernel, "block_two_rest", half(1), vmem(first_b, z_b, wo1, wu1, wd1, gains), [], 0, 4_000_000_000)
+    out_b, mg, wm = call(
+        fourth_kernel, "block_two_rest", [jax.ShapeDtypeStruct((3, 9, LEV, 1024), BF16)] + MERGE,
+        vmem(first_b, z_b, wo1, wu1, wd1, gains) + hbm(merge_gain.reshape(1, -1), w_merge), [], 2, 5_000_000_000)
     out, = call(
         fifth_kernel, "merge", [jax.ShapeDtypeStruct((6, 9, LEV, 1024), BF16)],
-        vmem(first_a, att_a, second_b, wo1, wu1, wd1, gains) + hbm(merge_gain.reshape(1, -1), w_merge),
-        MERGE, 2, 5_000_000_000)
+        vmem(first_a, att_a, out_b, wo1, wu1, wd1, gains, mg, wm), [], 0, 5_000_000_000)
     return out
 
 

time: 59.6 us -> 56.2 us (0.943)
  Pallas kernels: 36.2 us -> 34.4 us
  waiting for transfers between devices: 8.18 us -> 6.66 us
    pallas_call x6, Pallas kernels: 36.2 us -> 34.4 us  [call(): pl.pallas_call(kernel, out_shape=outs, in_specs=[pl.BlockSpec(memory_spac...]
    ppermute x5, waiting for transfers between devices: 8.18 us -> 6.66 us  [ring(): lax.ppermute(value, axis, [(i, (i + by) % length) for i in range(length)])]
  transfers between devices with their start and end apart: 5 -> 5, of which waited for: 1 -> 1; matrix products, arithmetic and copies ran while one was open for 0% -> 0% of each run, Pallas kernels for 37% -> 40%
where the time goes in v2:
time: 56.2 us; the launch traced here: 56.1 us
  Pallas kernels  34.4 us (61%)
  starting transfers between devices  13.6 us (24%)
  waiting for transfers between devices  6.66 us (12%)
  local copies, waits for them, and re-layouts  1.26 us (2%)
    pallas_call x6, Pallas kernels, call(): pl.pallas_call(kernel, out_shape=outs, in_specs=[pl.BlockSpec(memory_spac...  34.4 us
    ppermute x5, starting transfers between devices, ring(): lax.ppermute(value, axis, [(i, (i + by) % length) for i in range(length)])  13.6 us
    ppermute x5, waiting for transfers between devices, ring(): lax.ppermute(value, axis, [(i, (i + by) % length) for i in range(length)])  6.66 us
    slice x1, local copies, waits for them, and re-layouts, body(): after = ring(stream[:, :6], 'lat', -1)  1.26 us
  transfers between devices with their start and end apart: 5, of which 1 were waited for; matrix products, arithmetic and copies ran while one was open for 0% of the time, Pallas kernels for 40%

profile of v2, /device:TPU:0, one launch (start us, length us, event | category | flops | bytes accessed | tf_op | source)
XLA Modules:
  0.0 56.1 jit_solution(16678997532770947455)
XLA Ops:
  0.0 1.3 %fusion = (bf16[12,6,4,512]{3,2,1,0:T(4,128)(2,1)S(1)}, bf16[12,6,4,512]{3,2,1,0:T(4,128)(2,1)S(1)}) fusion(bf16[12,18,4,512]{3,2,1,0:T(4,128)(2,1)} %x_h.1), kind=kLoop, calls=%fused_computation.1 | loop fusion | bytes 1179648 | tf_op jit(solution)/shard_map/slice | solution.py:330
  1.3 4.1 %collective-permute-start.2 = (bf16[12,6,4,512]{3,2,1,0:T(4,128)(2,1)S(1)}, bf16[12,6,4,512]{3,2,1,0:T(4,128)(2,1)S(1)}, u32[]{:S(2)}, u32[]{:S(2)}) collective-permute-start(bf16[12,6,4,512]{3,2,1,0:T(4,128)(2,1)S(1)} %get-tuple-element.47), channel_id=1, source_target_pairs={{0,7},{1,0},{2,1},{3,2},{4,3},{5,4},{6,5},{7,6},{8,15},{9,8},{10,9... | collective-permute-start | bytes 884744 | tf_op jit(solution)/shard_map/ppermute | solution.py:324
  5.4 0.0 collective-permute-start.1
  5.4 9.5 %block_one.1 = (bf16[432,512]{1,0:T(8,128)(2,1)S(1)}, bf16[432,512]{1,0:T(8,128)(2,1)S(1)}, bf16[432,512]{1,0:T(8,128)(2,1)S(1)}, bf16[432,512]{1,0:T(8,128)(2,1...) custom-call(bf16[12,18,4,512]{3,2,1,0:T(4,128)(2,1)} %x_h.1, ...), custom_call_target="tpu_custom_call" | custom-call | flops 6000000000 | bytes 6000000 | tf_op jit(solution)/shard_map/block_one/pallas_call | solution.py:302
  14.9 5.6 %collective-permute-start = (bf16[432,512]{1,0:T(8,128)(2,1)S(1)}, bf16[432,512]{1,0:T(8,128)(2,1)S(1)}, u32[]{:S(2)}, u32[]{:S(2)}) collective-permute-start(bf16[432,512]{1,0:T(8,128)(2,1)S(1)} %get-tuple-element.34), channel_id=1, source_target_pairs={{0,120},{8,0},{16,8},{24,16},{32,24},{40,32},{48,40},{56,48},{64,5... | collective-permute-start | bytes 1327112 | tf_op jit(solution)/shard_map/ppermute | solution.py:324
  20.5 0.0 collective-permute-done.2.after
  20.5 0.0 collective-permute-done.1.before
  20.5 4.9 %block_one_beside.1 = (bf16[144,512]{1,0:T(8,128)(2,1)S(1)}, bf16[144,512]{1,0:T(8,128)(2,1)S(1)}) custom-call(bf16[12,6,4,512]{3,2,1,0:T(4,128)(2,1)S(1)} %collective-permute-done.1.before, bf16[12,6,4,512]{3,2,1,0:T(4,128)(2,1)S(1)} %collective-permute-done.2.after, bf16[512,1536]{1,0:T(8,128)(2,1)S(1)} %get-tuple-element.35.wqkv, ...), custom_call_target="tpu_custom_call" | custom-call | flops 4000000000 | bytes 6000000 | tf_op jit(solution)/shard_map/block_one_beside/pallas_call | solution.py:302
  25.4 3.6 %collective-permute-start.3 = (bf16[144,512]{1,0:T(8,128)(2,1)S(1)}, bf16[144,512]{1,0:T(8,128)(2,1)S(1)}, u32[]{:S(2)}, u32[]{:S(2)}) collective-permute-start(bf16[144,512]{1,0:T(8,128)(2,1)S(1)} %get-tuple-element.37), channel_id=1, source_target_pairs={{0,120},{8,0},{16,8},{24,16},{32,24},{40,32},{48,40},{56,48},{64,5... | collective-permute-start | bytes 442376 | tf_op jit(solution)/shard_map/ppermute | solution.py:324
  29.0 3.4 %block_one_rest.1 = (bf16[432,512]{1,0:T(8,128)(2,1)S(1)}, bf16[432,512]{1,0:T(8,128)(2,1)S(1)}) custom-call(bf16[432,512]{1,0:T(8,128)(2,1)S(1)} %get-tuple-element.27.x_b, bf16[432,512]{1,0:T(8,128)(2,1)S(1)} %get-tuple-element.28.att_b, bf16[512,512]{1,0:T(8,128)(2,1)S(1)} %get-tuple-element.29.wo, bf16[512,2048]{1,0:T(8,128)(2,1)S(1)} %get-tuple-element.30.wu, ...), custom_call_target="tpu_custom_call" | custom-call | flops 4000000000 | bytes 6000000 | tf_op jit(solution)/shard_map/block_one_rest/pallas_call | solution.py:302
  32.4 0.1 add_convert_fusion.edge
  32.5 0.0 collective-permute-done.3.halo_ra
  32.5 0.0 collective-permute-done.n_ra
  32.5 7.1 %shifted_attention.1 = (bf16[432,512]{1,0:T(8,128)(2,1)S(1)}, bf16[432,512]{1,0:T(8,128)(2,1)S(1)}, bf16[512,512]{1,0:T(8,128)(2,1)S(1)}, bf16[512,2048]{1,0:T(8,128)(2,1)S(1)}, bf16[2048,512]{1,0:T(8,128)(2,1)S(1)}) custom-call(s32[2]{0:T(128)S(1)} %add_convert_fusion.edge, bf16[432,512]{1,0:T(8,128)(2,1)S(1)} %get-tuple-element.33.n_b, ...), custom_call_target="tpu_custom_call" | custom-call | flops 4000000000 | bytes 6000000 | tf_op jit(solution)/shard_map/shifted_attention/pallas_call | solution.py:302
  39.6 0.3 collective-permute-start.4
  39.9 4.7 %block_two_rest.1 = (bf16[3,9,4,1024]{3,2,1,0:T(4,128)(2,1)S(1)}, f32[1,2048]{1,0:T(1,128)S(1)}, bf16[2048,1024]{1,0:T(8,128)(2,1)S(1)}) custom-call(bf16[432,512]{1,0:T(8,128)(2,1)S(1)} %get-tuple-element.39.f_b, bf16[432,512]{1,0:T(8,128)(2,1)S(1)} %get-tuple-element.40.att_b, bf16[512,512]{1,0:T(8,128)(2,1)S(1)} %get-tuple-element.41.wo, ...), custom_call_target="tpu_custom_call" | custom-call | flops 5000000000 | bytes 6000000 | tf_op jit(solution)/shard_map/block_two_rest/pallas_call | solution.py:302
  44.6 6.7 %collective-permute-done.4.att_a = bf16[432,512]{1,0:T(8,128)(2,1)S(1)} collective-permute-done((bf16[432,512]{1,0:T(8,128)(2,1)S(1)}, bf16[432,512]{1,0:T(8,128)(2,1)S(1)}, u32[]{:S(2)}, u32[]{:S(2)}) %collective-permute-start.4) | collective-permute-done | bytes 442400 | tf_op jit(solution)/shard_map/ppermute | solution.py:324
  51.2 4.9 %merge.1 = bf16[6,9,4,1024]{3,2,1,0:T(4,128)(2,1)} custom-call(bf16[432,512]{1,0:T(8,128)(2,1)S(1)} %get-tuple-element.26.f_a, bf16[432,512]{1,0:T(8,128)(2,1)S(1)} %collective-permute-done.4.att_a, bf16[3,9,4,1024]{3,2,1,0:T(4,128)(2,1)S(1)} %get-tuple-element.44.out_b, bf16[512,512]{1,0:T(8,128)(2,1)S(1)} %get-tuple-element.41.wo, ...), custom_call_target="tpu_custom_call" | custom-call | flops 5000000000 | bytes 6000000 | tf_op jit(solution)/shard_map/merge/pallas_call | solution.py:302
Async XLA Ops:
  1.3 19.2 %collective-permute-start.2 = (bf16[12,6,4,512]{3,2,1,0:T(4,128)(2,1)S(1)}, bf16[12,6,4,512]{3,2,1,0:T(4,128)(2,1)S(1)}, u32[]{:S(2)}, u32[]{:S(2)}) collective-permute-start(bf16[12,6,4,512]{3,2,1,0:T(4,128)(2,1)S(1)} %get-tuple-element.47), channel_id=1, source_target_pairs={{0,7},{1,0},{2,1},{3,2},{4,3},{5,4},{6,5},{7,6},{8,15},{9,8},{10,9... | collective-permute-start | bytes 884744 | tf_op jit(solution)/shard_map/ppermute | solution.py:324
  5.4 15.1 %collective-permute-start.1 = (bf16[12,6,4,512]{3,2,1,0:T(4,128)(2,1)S(1)}, bf16[12,6,4,512]{3,2,1,0:T(4,128)(2,1)S(1)}, u32[]{:S(2)}, u32[]{:S(2)}) collective-permute-start(bf16[12,6,4,512]{3,2,1,0:T(4,128)(2,1)S(1)} %get-tuple-element.48), channel_id=1, source_target_pairs={{0,1},{1,2},{2,3},{3,4},{4,5},{5,6},{6,7},{7,0},{8,9},{9,10},{10,1... | collective-permute-start | bytes 884744 | tf_op jit(solution)/shard_map/ppermute | solution.py:324
  14.9 17.6 %collective-permute-start = (bf16[432,512]{1,0:T(8,128)(2,1)S(1)}, bf16[432,512]{1,0:T(8,128)(2,1)S(1)}, u32[]{:S(2)}, u32[]{:S(2)}) collective-permute-start(bf16[432,512]{1,0:T(8,128)(2,1)S(1)} %get-tuple-element.34), channel_id=1, source_target_pairs={{0,120},{8,0},{16,8},{24,16},{32,24},{40,32},{48,40},{56,48},{64,5... | collective-permute-start | bytes 1327112 | tf_op jit(solution)/shard_map/ppermute | solution.py:324
  25.4 7.0 %collective-permute-start.3 = (bf16[144,512]{1,0:T(8,128)(2,1)S(1)}, bf16[144,512]{1,0:T(8,128)(2,1)S(1)}, u32[]{:S(2)}, u32[]{:S(2)}) collective-permute-start(bf16[144,512]{1,0:T(8,128)(2,1)S(1)} %get-tuple-element.37), channel_id=1, source_target_pairs={{0,120},{8,0},{16,8},{24,16},{32,24},{40,32},{48,40},{56,48},{64,5... | collective-permute-start | bytes 442376 | tf_op jit(solution)/shard_map/ppermute | solution.py:324
  39.6 11.6 %collective-permute-start.4 = (bf16[432,512]{1,0:T(8,128)(2,1)S(1)}, bf16[432,512]{1,0:T(8,128)(2,1)S(1)}, u32[]{:S(2)}, u32[]{:S(2)}) collective-permute-start(bf16[432,512]{1,0:T(8,128)(2,1)S(1)} %get-tuple-element.38), channel_id=1, source_target_pairs={{0,8},{8,16},{16,24},{24,32},{32,40},{40,48},{48,56},{56,64},{64,7... | collective-permute-start | bytes 1327112 | tf_op jit(solution)/shard_map/ppermute | solution.py:324

commit v3 on v2

--- a/solution.py
+++ b/solution.py
@@ -60,8 +60,15 @@
     return out
 
 
+def middle_rows(stream, attended, wo):
+    return round_bf16(stream + mm(attended, wo[...]))
+
+
 def finish_rows(stream, attended, wo, wu, wd, gain):
-    middle = round_bf16(stream + mm(attended, wo[...]))
+    return feed_rows(middle_rows(stream, attended, wo), wu, wd, gain)
+
+
+def feed_rows(middle, wu, wd, gain):
     hidden_in = norm_rows(middle, gain).astype(BF16)
     total = middle
     for c in range(4):
@@ -135,9 +142,11 @@
     return jnp.concatenate([ref[j] for j in range(4)], axis=1)
 
 
-def take_stream(x, dst, at, rows):
-    for r in range(rows):
-        for p in range(6):
+def take_stream(x, dst, at, rows, copies=None):
+    for p in range(6):
+        if copies is not None:
+            wait(copies[p])
+        for r in range(rows):
             pair = jnp.concatenate([x[2 * p, r].astype(F32), x[2 * p + 1, r].astype(F32)], axis=0)
             put_rows(dst, at + r * 48 + p * 8, pair)
 
@@ -145,22 +154,22 @@
 PLAIN = [window_runs(i * 288, levels, None) for levels in ((0, 1), (2, 3)) for i in range(3)]
 
 
-def first_kernel(x_h, wqkv_h, wo_h, wu_h, wd_h, gains_h, first_a, normed_a, x_b, att_b, wqkv, wo, wu, wd, gains,
+def first_kernel(x_h, wqkv_h, wo_h, wu_h, wd_h, gains_h, first_a, normed_a, middle_b, wqkv, wo, wu, wd, gains,
                  x, xs, ns, nw, packed, sems):
-    early = load(sems, (x_h, x), (gains_h, gains), (wqkv_h.at[0], wqkv))
-    wait(*early[:2])
-    take_stream(x, xs, 0, ROWS)
+    pairs = [(x_h.at[pl.ds(2 * p, 2)], x.at[pl.ds(2 * p, 2)]) for p in range(6)]
+    early = load(sems, *pairs, (gains_h, gains), (wqkv_h.at[0], wqkv))
+    take_stream(x, xs, 0, ROWS, early)
+    wait(early[6])
     put_rows(ns, 0, norm_rows(lanes(xs), gains[0, 0:1]))
     gather_windows(ns, nw, PLAIN)
-    wait(early[2])
-    copies = load(sems.at[6:], (wo_h.at[0], wo), (wu_h.at[0], wu), (wd_h.at[0], wd))
+    wait(early[7])
+    copies = load(sems.at[11:], (wo_h.at[0], wo), (wu_h.at[0], wu), (wd_h.at[0], wd))
     project(nw, packed, wqkv)
     for w, runs in enumerate(PLAIN):
         for group in range(2):
             scatter_run(ns, group, runs, attend_unit(packed, w * WIN, WIN, group, None))
-    x_b[...] = half_of(xs, 1).astype(BF16)
-    att_b[...] = half_of(ns, 1).astype(BF16)
     wait(*copies)
+    middle_b[...] = middle_rows(half_of(xs, 1), half_of(ns, 1).astype(BF16), wo).astype(BF16)
     result = finish_rows(half_of(xs, 0), half_of(ns, 0).astype(BF16), wo, wu, wd, gains[0, 1:2])
     first_a[...] = result.astype(BF16)
     normed_a[...] = norm_rows(result, gains[1, 0:1]).astype(BF16)
@@ -191,8 +200,8 @@
     halo_b[...] = near[:, 24:48].reshape(144, D).astype(BF16)
 
 
-def second_kernel(x_b, att_b, wo, wu, wd, gains, first_b, normed_b):
-    result = finish_rows(x_b[...].astype(F32), att_b[...], wo, wu, wd, gains[0, 1:2])
+def second_kernel(middle_b, wu, wd, gains, first_b, normed_b):
+    result = feed_rows(middle_b[...].astype(F32), wu, wd, gains[0, 1:2])
     first_b[...] = result.astype(BF16)
     normed_b[...] = norm_rows(result, gains[1, 0:1]).astype(BF16)
 
@@ -329,16 +338,16 @@
     edge = jnp.stack([place == 0, place == lax.axis_size("lat") - 1]).astype(jnp.int32)
     after = ring(stream[:, :6], "lat", -1)
     before = ring(stream[:, 12:], "lat", 1)
-    first_a, normed_a, x_b, att_b, wqkv0, wo0, wu0, wd0, gains = call(
-        first_kernel, "block_one", half(4) + QKV + FINISH + GAINS, hbm(stream, w_qkv, w_out, w_up, w_down, gains),
-        [pltpu.VMEM((COLS, ROWS, LEV, D), BF16), rows_f32(ALL)] + attention_scratch(ALL), 6, 6_000_000_000)
+    first_a, normed_a, middle_b, wqkv0, wo0, wu0, wd0, gains = call(
+        first_kernel, "block_one", half(3) + QKV + FINISH + GAINS, hbm(stream, w_qkv, w_out, w_up, w_down, gains),
+        [pltpu.VMEM((COLS, ROWS, LEV, D), BF16), rows_f32(ALL)] + attention_scratch(ALL), 8, 6_000_000_000)
     normed_ra = ring(normed_a, "lon", -1)
     halo_a, halo_b = call(
         halo_kernel, "block_one_beside", [pltpu.VMEM((144, D), BF16)] * 2,
         vmem(before, after, wqkv0, wo0, wu0, wd0, gains), [rows_f32(576)] + attention_scratch(576), 0, 4_000_000_000)
     halo_ra = ring(halo_a, "lon", -1)
     first_b, normed_b = call(
-        second_kernel, "block_one_rest", half(2), vmem(x_b, att_b, wo0, wu0, wd0, gains), [], 0, 4_000_000_000)
+        second_kernel, "block_one_rest", half(2), vmem(middle_b, wu0, wd0, gains), [], 0, 4_000_000_000)
     z_b, z_ra, wo1, wu1, wd1 = call(
         third_kernel, "shifted_attention", half(2) + FINISH,
         [(edge, pltpu.SMEM)] + vmem(normed_b, normed_ra, halo_b, halo_ra) + hbm(w_qkv, w_out, w_up, w_down),

time: 56.2 us -> 55.8 us (level)
  no operation moved by 1% of the time
where the time goes in v3:
time: 55.8 us; the launch traced here: 55.6 us
  Pallas kernels  34.2 us (61%)
  starting transfers between devices  13.3 us (24%)
  waiting for transfers between devices  6.66 us (12%)
  local copies, waits for them, and re-layouts  1.26 us (2%)
    pallas_call x6, Pallas kernels, call(): pl.pallas_call(kernel, out_shape=outs, in_specs=[pl.BlockSpec(memory_spac...  34.2 us
    ppermute x5, starting transfers between devices, ring(): lax.ppermute(value, axis, [(i, (i + by) % length) for i in range(length)])  13.3 us
    ppermute x5, waiting for transfers between devices, ring(): lax.ppermute(value, axis, [(i, (i + by) % length) for i in range(length)])  6.66 us
    slice x1, local copies, waits for them, and re-layouts, body(): after = ring(stream[:, :6], 'lat', -1)  1.26 us
  transfers between devices with their start and end apart: 5, of which 1 were waited for; matrix products, arithmetic and copies ran while one was open for 0% of the time, Pallas kernels for 40%

profile of v3, /device:TPU:0, one launch (start us, length us, event | category | flops | bytes accessed | tf_op | source)
XLA Modules:
  0.0 55.6 jit_solution(3119887613541714278)
XLA Ops:
  0.0 1.3 %fusion = (bf16[12,6,4,512]{3,2,1,0:T(4,128)(2,1)S(1)}, bf16[12,6,4,512]{3,2,1,0:T(4,128)(2,1)S(1)}) fusion(bf16[12,18,4,512]{3,2,1,0:T(4,128)(2,1)} %x_h.1), kind=kLoop, calls=%fused_computation.1 | loop fusion | bytes 1179648 | tf_op jit(solution)/shard_map/slice | solution.py:339
  1.3 4.1 %collective-permute-start.2 = (bf16[12,6,4,512]{3,2,1,0:T(4,128)(2,1)S(1)}, bf16[12,6,4,512]{3,2,1,0:T(4,128)(2,1)S(1)}, u32[]{:S(2)}, u32[]{:S(2)}) collective-permute-start(bf16[12,6,4,512]{3,2,1,0:T(4,128)(2,1)S(1)} %get-tuple-element.45), channel_id=1, source_target_pairs={{0,7},{1,0},{2,1},{3,2},{4,3},{5,4},{6,5},{7,6},{8,15},{9,8},{10,9... | collective-permute-start | bytes 884744 | tf_op jit(solution)/shard_map/ppermute | solution.py:333
  5.4 0.0 collective-permute-start.1
  5.4 9.7 %block_one.1 = (bf16[432,512]{1,0:T(8,128)(2,1)S(1)}, bf16[432,512]{1,0:T(8,128)(2,1)S(1)}, bf16[432,512]{1,0:T(8,128)(2,1)S(1)}, bf16[512,1536]{1,0:T(8,128)(2,...) custom-call(bf16[12,18,4,512]{3,2,1,0:T(4,128)(2,1)} %x_h.1, ...), custom_call_target="tpu_custom_call" | custom-call | flops 6000000000 | bytes 6000000 | tf_op jit(solution)/shard_map/block_one/pallas_call | solution.py:311
  15.1 5.6 %collective-permute-start = (bf16[432,512]{1,0:T(8,128)(2,1)S(1)}, bf16[432,512]{1,0:T(8,128)(2,1)S(1)}, u32[]{:S(2)}, u32[]{:S(2)}) collective-permute-start(bf16[432,512]{1,0:T(8,128)(2,1)S(1)} %get-tuple-element.31), channel_id=1, source_target_pairs={{0,120},{8,0},{16,8},{24,16},{32,24},{40,32},{48,40},{56,48},{64,5... | collective-permute-start | bytes 1327112 | tf_op jit(solution)/shard_map/ppermute | solution.py:333
  20.7 0.0 collective-permute-done.2.after
  20.7 0.0 collective-permute-done.1.before
  20.7 4.9 %block_one_beside.1 = (bf16[144,512]{1,0:T(8,128)(2,1)S(1)}, bf16[144,512]{1,0:T(8,128)(2,1)S(1)}) custom-call(bf16[12,6,4,512]{3,2,1,0:T(4,128)(2,1)S(1)} %collective-permute-done.1.before, bf16[12,6,4,512]{3,2,1,0:T(4,128)(2,1)S(1)} %collective-permute-done.2.after, bf16[512,1536]{1,0:T(8,128)(2,1)S(1)} %get-tuple-element.32.wqkv, ...), custom_call_target="tpu_custom_call" | custom-call | flops 4000000000 | bytes 6000000 | tf_op jit(solution)/shard_map/block_one_beside/pallas_call | solution.py:311
  25.7 3.3 %collective-permute-start.3 = (bf16[144,512]{1,0:T(8,128)(2,1)S(1)}, bf16[144,512]{1,0:T(8,128)(2,1)S(1)}, u32[]{:S(2)}, u32[]{:S(2)}) collective-permute-start(bf16[144,512]{1,0:T(8,128)(2,1)S(1)} %get-tuple-element.35), channel_id=1, source_target_pairs={{0,120},{8,0},{16,8},{24,16},{32,24},{40,32},{48,40},{56,48},{64,5... | collective-permute-start | bytes 442376 | tf_op jit(solution)/shard_map/ppermute | solution.py:333
  29.0 3.0 %block_one_rest.1 = (bf16[432,512]{1,0:T(8,128)(2,1)S(1)}, bf16[432,512]{1,0:T(8,128)(2,1)S(1)}) custom-call(bf16[432,512]{1,0:T(8,128)(2,1)S(1)} %get-tuple-element.26.middle_b, bf16[512,2048]{1,0:T(8,128)(2,1)S(1)} %get-tuple-element.27.wu, bf16[2048,512]{1,0:T(8,128)(2,1)S(1)} %get-tuple-element.28.wd, f32[2,2,512]{2,1,0:T(2,128)S(1)} %get-tuple-element.29.gains), custom_call_target="tpu_custom_call" | custom-call | flops 4000000000 | bytes 6000000 | tf_op jit(solution)/shard_map/block_one_rest/pallas_call | solution.py:311
  32.0 0.1 add_convert_fusion.edge
  32.0 0.0 collective-permute-done.3.halo_ra
  32.0 0.0 collective-permute-done.n_ra
  32.0 7.1 %shifted_attention.1 = (bf16[432,512]{1,0:T(8,128)(2,1)S(1)}, bf16[432,512]{1,0:T(8,128)(2,1)S(1)}, bf16[512,512]{1,0:T(8,128)(2,1)S(1)}, bf16[512,2048]{1,0:T(8,128)(2,1)S(1)}, bf16[2048,512]{1,0:T(8,128)(2,1)S(1)}) custom-call(s32[2]{0:T(128)S(1)} %add_convert_fusion.edge, bf16[432,512]{1,0:T(8,128)(2,1)S(1)} %get-tuple-element.30.n_b, ...), custom_call_target="tpu_custom_call" | custom-call | flops 4000000000 | bytes 6000000 | tf_op jit(solution)/shard_map/shifted_attention/pallas_call | solution.py:311
  39.1 0.3 collective-permute-start.4
  39.4 4.7 %block_two_rest.1 = (bf16[3,9,4,1024]{3,2,1,0:T(4,128)(2,1)S(1)}, f32[1,2048]{1,0:T(1,128)S(1)}, bf16[2048,1024]{1,0:T(8,128)(2,1)S(1)}) custom-call(bf16[432,512]{1,0:T(8,128)(2,1)S(1)} %get-tuple-element.37.f_b, bf16[432,512]{1,0:T(8,128)(2,1)S(1)} %get-tuple-element.38.att_b, bf16[512,512]{1,0:T(8,128)(2,1)S(1)} %get-tuple-element.39.wo, ...), custom_call_target="tpu_custom_call" | custom-call | flops 5000000000 | bytes 6000000 | tf_op jit(solution)/shard_map/block_two_rest/pallas_call | solution.py:311
  44.1 6.7 %collective-permute-done.4.att_a = bf16[432,512]{1,0:T(8,128)(2,1)S(1)} collective-permute-done((bf16[432,512]{1,0:T(8,128)(2,1)S(1)}, bf16[432,512]{1,0:T(8,128)(2,1)S(1)}, u32[]{:S(2)}, u32[]{:S(2)}) %collective-permute-start.4) | collective-permute-done | bytes 442400 | tf_op jit(solution)/shard_map/ppermute | solution.py:333
  50.8 4.9 %merge.1 = bf16[6,9,4,1024]{3,2,1,0:T(4,128)(2,1)} custom-call(bf16[432,512]{1,0:T(8,128)(2,1)S(1)} %get-tuple-element.25.f_a, bf16[432,512]{1,0:T(8,128)(2,1)S(1)} %collective-permute-done.4.att_a, bf16[3,9,4,1024]{3,2,1,0:T(4,128)(2,1)S(1)} %get-tuple-element.42.out_b, bf16[512,512]{1,0:T(8,128)(2,1)S(1)} %get-tuple-element.39.wo, ...), custom_call_target="tpu_custom_call" | custom-call | flops 5000000000 | bytes 6000000 | tf_op jit(solution)/shard_map/merge/pallas_call | solution.py:311
Async XLA Ops:
  1.3 19.5 %collective-permute-start.2 = (bf16[12,6,4,512]{3,2,1,0:T(4,128)(2,1)S(1)}, bf16[12,6,4,512]{3,2,1,0:T(4,128)(2,1)S(1)}, u32[]{:S(2)}, u32[]{:S(2)}) collective-permute-start(bf16[12,6,4,512]{3,2,1,0:T(4,128)(2,1)S(1)} %get-tuple-element.45), channel_id=1, source_target_pairs={{0,7},{1,0},{2,1},{3,2},{4,3},{5,4},{6,5},{7,6},{8,15},{9,8},{10,9... | collective-permute-start | bytes 884744 | tf_op jit(solution)/shard_map/ppermute | solution.py:333
  5.4 15.4 %collective-permute-start.1 = (bf16[12,6,4,512]{3,2,1,0:T(4,128)(2,1)S(1)}, bf16[12,6,4,512]{3,2,1,0:T(4,128)(2,1)S(1)}, u32[]{:S(2)}, u32[]{:S(2)}) collective-permute-start(bf16[12,6,4,512]{3,2,1,0:T(4,128)(2,1)S(1)} %get-tuple-element.46), channel_id=1, source_target_pairs={{0,1},{1,2},{2,3},{3,4},{4,5},{5,6},{6,7},{7,0},{8,9},{9,10},{10,1... | collective-permute-start | bytes 884744 | tf_op jit(solution)/shard_map/ppermute | solution.py:333
  15.1 16.9 %collective-permute-start = (bf16[432,512]{1,0:T(8,128)(2,1)S(1)}, bf16[432,512]{1,0:T(8,128)(2,1)S(1)}, u32[]{:S(2)}, u32[]{:S(2)}) collective-permute-start(bf16[432,512]{1,0:T(8,128)(2,1)S(1)} %get-tuple-element.31), channel_id=1, source_target_pairs={{0,120},{8,0},{16,8},{24,16},{32,24},{40,32},{48,40},{56,48},{64,5... | collective-permute-start | bytes 1327112 | tf_op jit(solution)/shard_map/ppermute | solution.py:333
  25.7 6.4 %collective-permute-start.3 = (bf16[144,512]{1,0:T(8,128)(2,1)S(1)}, bf16[144,512]{1,0:T(8,128)(2,1)S(1)}, u32[]{:S(2)}, u32[]{:S(2)}) collective-permute-start(bf16[144,512]{1,0:T(8,128)(2,1)S(1)} %get-tuple-element.35), channel_id=1, source_target_pairs={{0,120},{8,0},{16,8},{24,16},{32,24},{40,32},{48,40},{56,48},{64,5... | collective-permute-start | bytes 442376 | tf_op jit(solution)/shard_map/ppermute | solution.py:333
  39.1 11.6 %collective-permute-start.4 = (bf16[432,512]{1,0:T(8,128)(2,1)S(1)}, bf16[432,512]{1,0:T(8,128)(2,1)S(1)}, u32[]{:S(2)}, u32[]{:S(2)}) collective-permute-start(bf16[432,512]{1,0:T(8,128)(2,1)S(1)} %get-tuple-element.36), channel_id=1, source_target_pairs={{0,8},{8,16},{16,24},{24,32},{32,40},{40,48},{48,56},{56,64},{64,7... | collective-permute-start | bytes 1327112 | tf_op jit(solution)/shard_map/ppermute | solution.py:333

commit v4 on v3

--- a/solution.py
+++ b/solution.py
@@ -138,8 +138,8 @@
             copy.wait()
 
 
-def lanes(ref):
-    return jnp.concatenate([ref[j] for j in range(4)], axis=1)
+def lanes(ref, rows):
+    return jnp.concatenate([ref[j, 0:rows, :] for j in range(4)], axis=1)
 
 
 def take_stream(x, dst, at, rows, copies=None):
@@ -160,7 +160,7 @@
     early = load(sems, *pairs, (gains_h, gains), (wqkv_h.at[0], wqkv))
     take_stream(x, xs, 0, ROWS, early)
     wait(early[6])
-    put_rows(ns, 0, norm_rows(lanes(xs), gains[0, 0:1]))
+    put_rows(ns, 0, norm_rows(lanes(xs, ALL), gains[0, 0:1]))
     gather_windows(ns, nw, PLAIN)
     wait(early[7])
     copies = load(sems.at[11:], (wo_h.at[0], wo), (wu_h.at[0], wu), (wd_h.at[0], wd))
@@ -181,7 +181,7 @@
 def halo_kernel(before, after, wqkv, wo, wu, wd, gains, halo_a, halo_b, xs, ns, nw, packed):
     take_stream(before, xs, 0, 6)
     take_stream(after, xs, 288, 6)
-    put_rows(ns, 0, norm_rows(lanes(xs), gains[0, 0:1]))
+    put_rows(ns, 0, norm_rows(lanes(xs, 576), gains[0, 0:1]))
     gather_windows(ns, nw, BESIDE)
     project(nw, packed, wqkv)
     attended, stream = [], []
@@ -195,7 +195,7 @@
     for w, runs in enumerate(BESIDE):
         for group in range(2):
             scatter_run(ns, group, runs[:2], result[w * 72 : w * 72 + 72, group * 256 : group * 256 + 256])
-    near = jnp.concatenate([lanes(ns)[144:288], lanes(ns)[288:432]], axis=0).reshape(6, 48, D)
+    near = lanes(ns, 432)[144:].reshape(6, 48, D)
     halo_a[...] = near[:, 0:24].reshape(144, D).astype(BF16)
     halo_b[...] = near[:, 24:48].reshape(144, D).astype(BF16)
 
@@ -292,7 +292,7 @@
 
 
 def rows_f32(tokens):
-    return pltpu.VMEM((4, tokens, 128), F32)
+    return pltpu.VMEM((4, tokens + 32, 128), F32)
 
 
 def attention_scratch(tokens):

time: 55.8 us -> 55.8 us (level)
  no operation moved by 1% of the time
where the time goes in v4:
time: 55.8 us; the launch traced here: 55.6 us
  Pallas kernels  34.3 us (61%)
  starting transfers between devices  13.3 us (24%)
  waiting for transfers between devices  6.66 us (12%)
  local copies, waits for them, and re-layouts  1.26 us (2%)
    pallas_call x6, Pallas kernels, call(): pl.pallas_call(kernel, out_shape=outs, in_specs=[pl.BlockSpec(memory_spac...  34.3 us
    ppermute x5, starting transfers between devices, ring(): lax.ppermute(value, axis, [(i, (i + by) % length) for i in range(length)])  13.3 us
    ppermute x5, waiting for transfers between devices, ring(): lax.ppermute(value, axis, [(i, (i + by) % length) for i in range(length)])  6.66 us
    slice x1, local copies, waits for them, and re-layouts, body(): after = ring(stream[:, :6], 'lat', -1)  1.26 us
  transfers between devices with their start and end apart: 5, of which 1 were waited for; matrix products, arithmetic and copies ran while one was open for 0% of the time, Pallas kernels for 40%

profile of v4, /device:TPU:0, one launch (start us, length us, event | category | flops | bytes accessed | tf_op | source)
XLA Modules:
  0.0 55.6 jit_solution(2066591932165893822)
XLA Ops:
  0.0 1.3 %fusion = (bf16[12,6,4,512]{3,2,1,0:T(4,128)(2,1)S(1)}, bf16[12,6,4,512]{3,2,1,0:T(4,128)(2,1)S(1)}) fusion(bf16[12,18,4,512]{3,2,1,0:T(4,128)(2,1)} %x_h.1), kind=kLoop, calls=%fused_computation.1 | loop fusion | bytes 1179648 | tf_op jit(solution)/shard_map/slice | solution.py:339
  1.3 4.1 %collective-permute-start.2 = (bf16[12,6,4,512]{3,2,1,0:T(4,128)(2,1)S(1)}, bf16[12,6,4,512]{3,2,1,0:T(4,128)(2,1)S(1)}, u32[]{:S(2)}, u32[]{:S(2)}) collective-permute-start(bf16[12,6,4,512]{3,2,1,0:T(4,128)(2,1)S(1)} %get-tuple-element.45), channel_id=1, source_target_pairs={{0,7},{1,0},{2,1},{3,2},{4,3},{5,4},{6,5},{7,6},{8,15},{9,8},{10,9... | collective-permute-start | bytes 884744 | tf_op jit(solution)/shard_map/ppermute | solution.py:333
  5.4 0.0 collective-permute-start.1
  5.4 9.8 %block_one.1 = (bf16[432,512]{1,0:T(8,128)(2,1)S(1)}, bf16[432,512]{1,0:T(8,128)(2,1)S(1)}, bf16[432,512]{1,0:T(8,128)(2,1)S(1)}, bf16[512,1536]{1,0:T(8,128)(2,...) custom-call(bf16[12,18,4,512]{3,2,1,0:T(4,128)(2,1)} %x_h.1, ...), custom_call_target="tpu_custom_call" | custom-call | flops 6000000000 | bytes 6000000 | tf_op jit(solution)/shard_map/block_one/pallas_call | solution.py:311
  15.1 5.6 %collective-permute-start = (bf16[432,512]{1,0:T(8,128)(2,1)S(1)}, bf16[432,512]{1,0:T(8,128)(2,1)S(1)}, u32[]{:S(2)}, u32[]{:S(2)}) collective-permute-start(bf16[432,512]{1,0:T(8,128)(2,1)S(1)} %get-tuple-element.31), channel_id=1, source_target_pairs={{0,120},{8,0},{16,8},{24,16},{32,24},{40,32},{48,40},{56,48},{64,5... | collective-permute-start | bytes 1327112 | tf_op jit(solution)/shard_map/ppermute | solution.py:333
  20.8 0.0 collective-permute-done.2.after
  20.8 0.0 collective-permute-done.1.before
  20.8 4.9 %block_one_beside.1 = (bf16[144,512]{1,0:T(8,128)(2,1)S(1)}, bf16[144,512]{1,0:T(8,128)(2,1)S(1)}) custom-call(bf16[12,6,4,512]{3,2,1,0:T(4,128)(2,1)S(1)} %collective-permute-done.1.before, bf16[12,6,4,512]{3,2,1,0:T(4,128)(2,1)S(1)} %collective-permute-done.2.after, bf16[512,1536]{1,0:T(8,128)(2,1)S(1)} %get-tuple-element.32.wqkv, ...), custom_call_target="tpu_custom_call" | custom-call | flops 4000000000 | bytes 6000000 | tf_op jit(solution)/shard_map/block_one_beside/pallas_call | solution.py:311
  25.7 3.3 %collective-permute-start.3 = (bf16[144,512]{1,0:T(8,128)(2,1)S(1)}, bf16[144,512]{1,0:T(8,128)(2,1)S(1)}, u32[]{:S(2)}, u32[]{:S(2)}) collective-permute-start(bf16[144,512]{1,0:T(8,128)(2,1)S(1)} %get-tuple-element.35), channel_id=1, source_target_pairs={{0,120},{8,0},{16,8},{24,16},{32,24},{40,32},{48,40},{56,48},{64,5... | collective-permute-start | bytes 442376 | tf_op jit(solution)/shard_map/ppermute | solution.py:333
  29.0 3.0 %block_one_rest.1 = (bf16[432,512]{1,0:T(8,128)(2,1)S(1)}, bf16[432,512]{1,0:T(8,128)(2,1)S(1)}) custom-call(bf16[432,512]{1,0:T(8,128)(2,1)S(1)} %get-tuple-element.26.middle_b, bf16[512,2048]{1,0:T(8,128)(2,1)S(1)} %get-tuple-element.27.wu, bf16[2048,512]{1,0:T(8,128)(2,1)S(1)} %get-tuple-element.28.wd, f32[2,2,512]{2,1,0:T(2,128)S(1)} %get-tuple-element.29.gains), custom_call_target="tpu_custom_call" | custom-call | flops 4000000000 | bytes 6000000 | tf_op jit(solution)/shard_map/block_one_rest/pallas_call | solution.py:311
  32.0 0.1 add_convert_fusion.edge
  32.0 0.0 collective-permute-done.3.halo_ra
  32.0 0.0 collective-permute-done.n_ra
  32.0 7.1 %shifted_attention.1 = (bf16[432,512]{1,0:T(8,128)(2,1)S(1)}, bf16[432,512]{1,0:T(8,128)(2,1)S(1)}, bf16[512,512]{1,0:T(8,128)(2,1)S(1)}, bf16[512,2048]{1,0:T(8,128)(2,1)S(1)}, bf16[2048,512]{1,0:T(8,128)(2,1)S(1)}) custom-call(s32[2]{0:T(128)S(1)} %add_convert_fusion.edge, bf16[432,512]{1,0:T(8,128)(2,1)S(1)} %get-tuple-element.30.n_b, ...), custom_call_target="tpu_custom_call" | custom-call | flops 4000000000 | bytes 6000000 | tf_op jit(solution)/shard_map/shifted_attention/pallas_call | solution.py:311
  39.1 0.3 collective-permute-start.4
  39.4 4.7 %block_two_rest.1 = (bf16[3,9,4,1024]{3,2,1,0:T(4,128)(2,1)S(1)}, f32[1,2048]{1,0:T(1,128)S(1)}, bf16[2048,1024]{1,0:T(8,128)(2,1)S(1)}) custom-call(bf16[432,512]{1,0:T(8,128)(2,1)S(1)} %get-tuple-element.37.f_b, bf16[432,512]{1,0:T(8,128)(2,1)S(1)} %get-tuple-element.38.att_b, bf16[512,512]{1,0:T(8,128)(2,1)S(1)} %get-tuple-element.39.wo, ...), custom_call_target="tpu_custom_call" | custom-call | flops 5000000000 | bytes 6000000 | tf_op jit(solution)/shard_map/block_two_rest/pallas_call | solution.py:311
  44.1 6.7 %collective-permute-done.4.att_a = bf16[432,512]{1,0:T(8,128)(2,1)S(1)} collective-permute-done((bf16[432,512]{1,0:T(8,128)(2,1)S(1)}, bf16[432,512]{1,0:T(8,128)(2,1)S(1)}, u32[]{:S(2)}, u32[]{:S(2)}) %collective-permute-start.4) | collective-permute-done | bytes 442400 | tf_op jit(solution)/shard_map/ppermute | solution.py:333
  50.8 4.9 %merge.1 = bf16[6,9,4,1024]{3,2,1,0:T(4,128)(2,1)} custom-call(bf16[432,512]{1,0:T(8,128)(2,1)S(1)} %get-tuple-element.25.f_a, bf16[432,512]{1,0:T(8,128)(2,1)S(1)} %collective-permute-done.4.att_a, bf16[3,9,4,1024]{3,2,1,0:T(4,128)(2,1)S(1)} %get-tuple-element.42.out_b, bf16[512,512]{1,0:T(8,128)(2,1)S(1)} %get-tuple-element.39.wo, ...), custom_call_target="tpu_custom_call" | custom-call | flops 5000000000 | bytes 6000000 | tf_op jit(solution)/shard_map/merge/pallas_call | solution.py:311
Async XLA Ops:
  1.3 19.5 %collective-permute-start.2 = (bf16[12,6,4,512]{3,2,1,0:T(4,128)(2,1)S(1)}, bf16[12,6,4,512]{3,2,1,0:T(4,128)(2,1)S(1)}, u32[]{:S(2)}, u32[]{:S(2)}) collective-permute-start(bf16[12,6,4,512]{3,2,1,0:T(4,128)(2,1)S(1)} %get-tuple-element.45), channel_id=1, source_target_pairs={{0,7},{1,0},{2,1},{3,2},{4,3},{5,4},{6,5},{7,6},{8,15},{9,8},{10,9... | collective-permute-start | bytes 884744 | tf_op jit(solution)/shard_map/ppermute | solution.py:333
  5.4 15.4 %collective-permute-start.1 = (bf16[12,6,4,512]{3,2,1,0:T(4,128)(2,1)S(1)}, bf16[12,6,4,512]{3,2,1,0:T(4,128)(2,1)S(1)}, u32[]{:S(2)}, u32[]{:S(2)}) collective-permute-start(bf16[12,6,4,512]{3,2,1,0:T(4,128)(2,1)S(1)} %get-tuple-element.46), channel_id=1, source_target_pairs={{0,1},{1,2},{2,3},{3,4},{4,5},{5,6},{6,7},{7,0},{8,9},{9,10},{10,1... | collective-permute-start | bytes 884744 | tf_op jit(solution)/shard_map/ppermute | solution.py:333
  15.1 16.9 %collective-permute-start = (bf16[432,512]{1,0:T(8,128)(2,1)S(1)}, bf16[432,512]{1,0:T(8,128)(2,1)S(1)}, u32[]{:S(2)}, u32[]{:S(2)}) collective-permute-start(bf16[432,512]{1,0:T(8,128)(2,1)S(1)} %get-tuple-element.31), channel_id=1, source_target_pairs={{0,120},{8,0},{16,8},{24,16},{32,24},{40,32},{48,40},{56,48},{64,5... | collective-permute-start | bytes 1327112 | tf_op jit(solution)/shard_map/ppermute | solution.py:333
  25.7 6.4 %collective-permute-start.3 = (bf16[144,512]{1,0:T(8,128)(2,1)S(1)}, bf16[144,512]{1,0:T(8,128)(2,1)S(1)}, u32[]{:S(2)}, u32[]{:S(2)}) collective-permute-start(bf16[144,512]{1,0:T(8,128)(2,1)S(1)} %get-tuple-element.35), channel_id=1, source_target_pairs={{0,120},{8,0},{16,8},{24,16},{32,24},{40,32},{48,40},{56,48},{64,5... | collective-permute-start | bytes 442376 | tf_op jit(solution)/shard_map/ppermute | solution.py:333
  39.1 11.6 %collective-permute-start.4 = (bf16[432,512]{1,0:T(8,128)(2,1)S(1)}, bf16[432,512]{1,0:T(8,128)(2,1)S(1)}, u32[]{:S(2)}, u32[]{:S(2)}) collective-permute-start(bf16[432,512]{1,0:T(8,128)(2,1)S(1)} %get-tuple-element.36), channel_id=1, source_target_pairs={{0,8},{8,16},{16,24},{24,32},{32,40},{40,48},{48,56},{56,64},{64,7... | collective-permute-start | bytes 1327112 | tf_op jit(solution)/shard_map/ppermute | solution.py:333

commit v5 on v4

--- a/solution.py
+++ b/solution.py
@@ -35,8 +35,8 @@
 
 
 def gelu(x):
-    inner = 0.7978845608028654 * (x + 0.044715 * (x * x * x))
-    return 0.5 * x * (1.0 + jnp.tanh(inner))
+    half = 0.5 * x
+    return half + half * jnp.tanh(x * (0.7978845608028654 + 0.035677408136300125 * (x * x)))
 
 
 def attend_unit(packed_ref, row0, count, group, mask):

time: 55.8 us -> 55.9 us (level)
  no operation moved by 1% of the time
where the time goes in v5:
time: 55.9 us; the launch traced here: 55.7 us
  Pallas kernels  34.3 us (61%)
  starting transfers between devices  13.4 us (24%)
  waiting for transfers between devices  6.66 us (12%)
  local copies, waits for them, and re-layouts  1.26 us (2%)
    pallas_call x6, Pallas kernels, call(): pl.pallas_call(kernel, out_shape=outs, in_specs=[pl.BlockSpec(memory_spac...  34.3 us
    ppermute x5, starting transfers between devices, ring(): lax.ppermute(value, axis, [(i, (i + by) % length) for i in range(length)])  13.4 us
    ppermute x5, waiting for transfers between devices, ring(): lax.ppermute(value, axis, [(i, (i + by) % length) for i in range(length)])  6.66 us
    slice x1, local copies, waits for them, and re-layouts, body(): after = ring(stream[:, :6], 'lat', -1)  1.26 us
  transfers between devices with their start and end apart: 5, of which 1 were waited for; matrix products, arithmetic and copies ran while one was open for 0% of the time, Pallas kernels for 40%

profile of v5, /device:TPU:0, one launch (start us, length us, event | category | flops | bytes accessed | tf_op | source)
XLA Modules:
  0.0 55.7 jit_solution(5739341789091444606)
XLA Ops:
  0.0 1.3 %fusion = (bf16[12,6,4,512]{3,2,1,0:T(4,128)(2,1)S(1)}, bf16[12,6,4,512]{3,2,1,0:T(4,128)(2,1)S(1)}) fusion(bf16[12,18,4,512]{3,2,1,0:T(4,128)(2,1)} %x_h.1), kind=kLoop, calls=%fused_computation.1 | loop fusion | bytes 1179648 | tf_op jit(solution)/shard_map/slice | solution.py:339
  1.3 4.1 %collective-permute-start.2 = (bf16[12,6,4,512]{3,2,1,0:T(4,128)(2,1)S(1)}, bf16[12,6,4,512]{3,2,1,0:T(4,128)(2,1)S(1)}, u32[]{:S(2)}, u32[]{:S(2)}) collective-permute-start(bf16[12,6,4,512]{3,2,1,0:T(4,128)(2,1)S(1)} %get-tuple-element.45), channel_id=1, source_target_pairs={{0,7},{1,0},{2,1},{3,2},{4,3},{5,4},{6,5},{7,6},{8,15},{9,8},{10,9... | collective-permute-start | bytes 884744 | tf_op jit(solution)/shard_map/ppermute | solution.py:333
  5.4 0.0 collective-permute-start.1
  5.4 9.7 %block_one.1 = (bf16[432,512]{1,0:T(8,128)(2,1)S(1)}, bf16[432,512]{1,0:T(8,128)(2,1)S(1)}, bf16[432,512]{1,0:T(8,128)(2,1)S(1)}, bf16[512,1536]{1,0:T(8,128)(2,...) custom-call(bf16[12,18,4,512]{3,2,1,0:T(4,128)(2,1)} %x_h.1, ...), custom_call_target="tpu_custom_call" | custom-call | flops 6000000000 | bytes 6000000 | tf_op jit(solution)/shard_map/block_one/pallas_call | solution.py:311
  15.1 5.6 %collective-permute-start = (bf16[432,512]{1,0:T(8,128)(2,1)S(1)}, bf16[432,512]{1,0:T(8,128)(2,1)S(1)}, u32[]{:S(2)}, u32[]{:S(2)}) collective-permute-start(bf16[432,512]{1,0:T(8,128)(2,1)S(1)} %get-tuple-element.31), channel_id=1, source_target_pairs={{0,120},{8,0},{16,8},{24,16},{32,24},{40,32},{48,40},{56,48},{64,5... | collective-permute-start | bytes 1327112 | tf_op jit(solution)/shard_map/ppermute | solution.py:333
  20.7 0.0 collective-permute-done.2.after
  20.7 0.0 collective-permute-done.1.before
  20.7 4.9 %block_one_beside.1 = (bf16[144,512]{1,0:T(8,128)(2,1)S(1)}, bf16[144,512]{1,0:T(8,128)(2,1)S(1)}) custom-call(bf16[12,6,4,512]{3,2,1,0:T(4,128)(2,1)S(1)} %collective-permute-done.1.before, bf16[12,6,4,512]{3,2,1,0:T(4,128)(2,1)S(1)} %collective-permute-done.2.after, bf16[512,1536]{1,0:T(8,128)(2,1)S(1)} %get-tuple-element.32.wqkv, ...), custom_call_target="tpu_custom_call" | custom-call | flops 4000000000 | bytes 6000000 | tf_op jit(solution)/shard_map/block_one_beside/pallas_call | solution.py:311
  25.6 3.4 %collective-permute-start.3 = (bf16[144,512]{1,0:T(8,128)(2,1)S(1)}, bf16[144,512]{1,0:T(8,128)(2,1)S(1)}, u32[]{:S(2)}, u32[]{:S(2)}) collective-permute-start(bf16[144,512]{1,0:T(8,128)(2,1)S(1)} %get-tuple-element.35), channel_id=1, source_target_pairs={{0,120},{8,0},{16,8},{24,16},{32,24},{40,32},{48,40},{56,48},{64,5... | collective-permute-start | bytes 442376 | tf_op jit(solution)/shard_map/ppermute | solution.py:333
  29.0 3.0 %block_one_rest.1 = (bf16[432,512]{1,0:T(8,128)(2,1)S(1)}, bf16[432,512]{1,0:T(8,128)(2,1)S(1)}) custom-call(bf16[432,512]{1,0:T(8,128)(2,1)S(1)} %get-tuple-element.26.middle_b, bf16[512,2048]{1,0:T(8,128)(2,1)S(1)} %get-tuple-element.27.wu, bf16[2048,512]{1,0:T(8,128)(2,1)S(1)} %get-tuple-element.28.wd, f32[2,2,512]{2,1,0:T(2,128)S(1)} %get-tuple-element.29.gains), custom_call_target="tpu_custom_call" | custom-call | flops 4000000000 | bytes 6000000 | tf_op jit(solution)/shard_map/block_one_rest/pallas_call | solution.py:311
  32.0 0.1 add_convert_fusion.edge
  32.1 0.0 collective-permute-done.3.halo_ra
  32.1 0.0 collective-permute-done.n_ra
  32.1 7.1 %shifted_attention.1 = (bf16[432,512]{1,0:T(8,128)(2,1)S(1)}, bf16[432,512]{1,0:T(8,128)(2,1)S(1)}, bf16[512,512]{1,0:T(8,128)(2,1)S(1)}, bf16[512,2048]{1,0:T(8,128)(2,1)S(1)}, bf16[2048,512]{1,0:T(8,128)(2,1)S(1)}) custom-call(s32[2]{0:T(128)S(1)} %add_convert_fusion.edge, bf16[432,512]{1,0:T(8,128)(2,1)S(1)} %get-tuple-element.30.n_b, ...), custom_call_target="tpu_custom_call" | custom-call | flops 4000000000 | bytes 6000000 | tf_op jit(solution)/shard_map/shifted_attention/pallas_call | solution.py:311
  39.2 0.3 collective-permute-start.4
  39.5 4.7 %block_two_rest.1 = (bf16[3,9,4,1024]{3,2,1,0:T(4,128)(2,1)S(1)}, f32[1,2048]{1,0:T(1,128)S(1)}, bf16[2048,1024]{1,0:T(8,128)(2,1)S(1)}) custom-call(bf16[432,512]{1,0:T(8,128)(2,1)S(1)} %get-tuple-element.37.f_b, bf16[432,512]{1,0:T(8,128)(2,1)S(1)} %get-tuple-element.38.att_b, bf16[512,512]{1,0:T(8,128)(2,1)S(1)} %get-tuple-element.39.wo, ...), custom_call_target="tpu_custom_call" | custom-call | flops 5000000000 | bytes 6000000 | tf_op jit(solution)/shard_map/block_two_rest/pallas_call | solution.py:311
  44.2 6.7 %collective-permute-done.4.att_a = bf16[432,512]{1,0:T(8,128)(2,1)S(1)} collective-permute-done((bf16[432,512]{1,0:T(8,128)(2,1)S(1)}, bf16[432,512]{1,0:T(8,128)(2,1)S(1)}, u32[]{:S(2)}, u32[]{:S(2)}) %collective-permute-start.4) | collective-permute-done | bytes 442400 | tf_op jit(solution)/shard_map/ppermute | solution.py:333
  50.8 4.9 %merge.1 = bf16[6,9,4,1024]{3,2,1,0:T(4,128)(2,1)} custom-call(bf16[432,512]{1,0:T(8,128)(2,1)S(1)} %get-tuple-element.25.f_a, bf16[432,512]{1,0:T(8,128)(2,1)S(1)} %collective-permute-done.4.att_a, bf16[3,9,4,1024]{3,2,1,0:T(4,128)(2,1)S(1)} %get-tuple-element.42.out_b, bf16[512,512]{1,0:T(8,128)(2,1)S(1)} %get-tuple-element.39.wo, ...), custom_call_target="tpu_custom_call" | custom-call | flops 5000000000 | bytes 6000000 | tf_op jit(solution)/shard_map/merge/pallas_call | solution.py:311
Async XLA Ops:
  1.3 19.4 %collective-permute-start.2 = (bf16[12,6,4,512]{3,2,1,0:T(4,128)(2,1)S(1)}, bf16[12,6,4,512]{3,2,1,0:T(4,128)(2,1)S(1)}, u32[]{:S(2)}, u32[]{:S(2)}) collective-permute-start(bf16[12,6,4,512]{3,2,1,0:T(4,128)(2,1)S(1)} %get-tuple-element.45), channel_id=1, source_target_pairs={{0,7},{1,0},{2,1},{3,2},{4,3},{5,4},{6,5},{7,6},{8,15},{9,8},{10,9... | collective-permute-start | bytes 884744 | tf_op jit(solution)/shard_map/ppermute | solution.py:333
  5.4 15.4 %collective-permute-start.1 = (bf16[12,6,4,512]{3,2,1,0:T(4,128)(2,1)S(1)}, bf16[12,6,4,512]{3,2,1,0:T(4,128)(2,1)S(1)}, u32[]{:S(2)}, u32[]{:S(2)}) collective-permute-start(bf16[12,6,4,512]{3,2,1,0:T(4,128)(2,1)S(1)} %get-tuple-element.46), channel_id=1, source_target_pairs={{0,1},{1,2},{2,3},{3,4},{4,5},{5,6},{6,7},{7,0},{8,9},{9,10},{10,1... | collective-permute-start | bytes 884744 | tf_op jit(solution)/shard_map/ppermute | solution.py:333
  15.1 17.0 %collective-permute-start = (bf16[432,512]{1,0:T(8,128)(2,1)S(1)}, bf16[432,512]{1,0:T(8,128)(2,1)S(1)}, u32[]{:S(2)}, u32[]{:S(2)}) collective-permute-start(bf16[432,512]{1,0:T(8,128)(2,1)S(1)} %get-tuple-element.31), channel_id=1, source_target_pairs={{0,120},{8,0},{16,8},{24,16},{32,24},{40,32},{48,40},{56,48},{64,5... | collective-permute-start | bytes 1327112 | tf_op jit(solution)/shard_map/ppermute | solution.py:333
  25.6 6.5 %collective-permute-start.3 = (bf16[144,512]{1,0:T(8,128)(2,1)S(1)}, bf16[144,512]{1,0:T(8,128)(2,1)S(1)}, u32[]{:S(2)}, u32[]{:S(2)}) collective-permute-start(bf16[144,512]{1,0:T(8,128)(2,1)S(1)} %get-tuple-element.35), channel_id=1, source_target_pairs={{0,120},{8,0},{16,8},{24,16},{32,24},{40,32},{48,40},{56,48},{64,5... | collective-permute-start | bytes 442376 | tf_op jit(solution)/shard_map/ppermute | solution.py:333
  39.2 11.6 %collective-permute-start.4 = (bf16[432,512]{1,0:T(8,128)(2,1)S(1)}, bf16[432,512]{1,0:T(8,128)(2,1)S(1)}, u32[]{:S(2)}, u32[]{:S(2)}) collective-permute-start(bf16[432,512]{1,0:T(8,128)(2,1)S(1)} %get-tuple-element.36), channel_id=1, source_target_pairs={{0,8},{8,16},{16,24},{24,32},{32,40},{40,48},{48,56},{56,64},{64,7... | collective-permute-start | bytes 1327112 | tf_op jit(solution)/shard_map/ppermute | solution.py:333
